TPU v7x, 256 devices: a whole 4x4x8 slice. The times are simulated.
256 devices in a mesh: fibre: 16 (over z_lo, y, core), band: 16 (over x, z_hi).
Axes of the slice: x: 4, y: 4, z: 8 (z_hi: 4, z_lo: 2; z = z_hi * 2 + z_lo), core: 2. Of those that a mesh axis runs over, the one named last changes fastest.
Arguments:
- spectra: bfloat16 [2, 32, 512, 2048], P(None, None, 'band', 'fibre'), may hold values from -6 to 6
- dead_mask: int32 [2048], P('fibre'), may hold values 0 or 1
- partner_offset: int32 [16, 4], P('fibre'), may hold values from 0 to 8, as said below
Outputs:
- correlations: bfloat16 [32, 16, 4, 128, 128], P('band', 'fibre')
Inputs may be any that keep to these rules, and one draw needn't show every extreme that they name: `partner_offset`: A block's partner is itself or a later block, never past the last block; slot 0 holds the farthest partner allowed, min(8, 15 - b).
All inputs are finite; a program needn't handle non-finite values. No bound on the sum of `dead_mask` on one device may be relied on, other than what follows from the above.
Results may differ from a plain program's by a relative error of at most 0.0045.
Values may be sent and summed in bfloat16 or wider, within the bound.
A program may use at most 128 MiB of HBM per device.

v0:
```python
import math

import jax
import jax.numpy as jnp
from jax import lax
from jax.sharding import PartitionSpec as P

BS = 128
NF = 512
REACH = 8
K = 4
LAGS = 32


def from_behind(value, axis, steps):
    count = lax.axis_size(axis)
    initial, last = (max(0, -steps), min(count, count - steps))
    return lax.ppermute(value, axis, [(source, source + steps) for source in range(initial, last)])


def make_table(freq_index):
    lag_index = jnp.arange(LAGS, dtype=jnp.int32) - LAGS // 2
    phases = freq_index[:, None] * lag_index[None, :] % (2 * NF)
    angles = phases.astype(jnp.float32) * (math.pi / NF)
    return jnp.stack([jnp.cos(angles), -jnp.sin(angles)], axis=1).astype(jnp.bfloat16)


def on_device(spectra, dead_mask, partner_offset):
    masked = spectra * dead_mask.astype(jnp.bfloat16)[None, None, None, :]
    blocks_here = partner_offset.shape[0]
    windows = spectra.shape[1]
    bins_here = spectra.shape[2]
    fibre_count = lax.axis_size("fibre")
    reach_hops = min((REACH + blocks_here - 1) // blocks_here, fibre_count - 1)
    pieces = [masked]
    for distance in range(1, reach_hops + 1):
        pieces.append(from_behind(masked, "fibre", -distance))
    extended = jnp.concatenate(pieces, axis=3)
    right_all = extended.reshape(2 * windows, bins_here, extended.shape[3])
    block_start = (jnp.arange(blocks_here, dtype=jnp.int32)[:, None] + partner_offset) * BS
    columns = (block_start[:, :, None] + jnp.arange(BS, dtype=jnp.int32)[None, None, :]).reshape(-1)
    partners = jnp.take(right_all, columns, axis=2).reshape(
        2 * windows, bins_here, blocks_here, K * BS
    )
    own_real = masked.reshape(2 * windows, bins_here, blocks_here, BS)
    own_imag = jnp.concatenate([masked[1], -masked[0]], axis=0).reshape(
        2 * windows, bins_here, blocks_here, BS
    )
    left_side = jnp.stack([own_real, own_imag], axis=3).reshape(
        2 * windows, bins_here, blocks_here, 2 * BS
    )
    products = jnp.einsum(
        "wfbi,wfbj->fbij", left_side, partners, preferred_element_type=jnp.float32
    )
    cross = (products * (1.0 / math.sqrt(windows))).astype(jnp.bfloat16)
    cross = cross.reshape(bins_here, blocks_here, 2, BS, K, BS).transpose(0, 2, 1, 4, 3, 5)
    cross = cross.reshape(bins_here, 2, blocks_here * K, BS * BS)
    band_count = lax.axis_size("band")
    lags_here = LAGS // band_count
    scale = 1.0 / math.sqrt(NF)
    freq_index = lax.axis_index("band") * bins_here + jnp.arange(bins_here, dtype=jnp.int32)
    local_table = make_table(freq_index)
    flat_cross = cross.reshape(bins_here, 2, blocks_here * K * BS * BS)
    summed = lax.psum_scatter(
        jnp.einsum("frl,frx->lx", local_table, flat_cross, preferred_element_type=jnp.float32),
        "band",
        scatter_dimension=0,
        tiled=True,
    )
    lagged = (summed * scale).astype(jnp.bfloat16)
    return lagged.reshape(lags_here, blocks_here, K, BS, BS)


def solution(mesh):
    in_specs = (P(None, None, "band", "fibre"), P("fibre"), P("fibre", None))
    out_specs = P("band", "fibre", None, None, None)
    return jax.shard_map(
        on_device, mesh=mesh, in_specs=in_specs, out_specs=out_specs, check_vma=False
    )
```

profile of v0, /device:TPU:9, one launch (start us, length us, event | category | flops | bytes accessed | tf_op | source)
XLA Modules:
  0.0 600.0 jit_solution(18244585463282601164)
XLA Ops:
  6.5 0.7 convert_element_type.26
  7.2 2.0 constant_dynamic-update-slice_fusion.8
  9.2 2.6 collective-permute-start
  11.8 3.8 collective-permute-start.1
  15.6 1.9 collective-permute-start.2
  17.6 1.3 collective-permute-start.3
  18.9 1.3 collective-permute-start.4
  20.2 0.1 slice_bitcast_fusion
  20.2 0.7 multiply_bitcast_fusion
  20.9 0.1 compare_select_fusion
  21.0 0.2 cosine_convert_fusion
  21.1 0.1 add.95
  21.3 0.1 pad_maximum_fusion
  21.4 1.1 copy.17
  22.5 0.7 reshape.207
  23.2 0.4 collective-permute-done
  23.6 1.3 collective-permute-start.5
  24.9 1.9 constant_dynamic-update-slice_fusion.7
  26.8 9.8 %collective-permute-done.1 = bf16[2,32,32,128]{3,2,1,0:T(8,128)(2,1)} collective-permute-done((bf16[2,32,32,128]{3,2,1,0:T(8,128)(2,1)S(1)}, bf16[2,32,32,128]{3,2,1,0:T(8,128)(2,1)}, u32[]{:S(2)}, u32[]{:S(2)}) %collective-permute-start.1) | collective-permute-done | bytes 524320 | tf_op jit(solution)/shard_map/ppermute | solution.py:18
  36.6 1.3 collective-permute-start.6
  37.9 1.9 constant_dynamic-update-slice_fusion.6
  39.8 14.0 %collective-permute-done.2 = bf16[2,32,32,128]{3,2,1,0:T(8,128)(2,1)} collective-permute-done((bf16[2,32,32,128]{3,2,1,0:T(8,128)(2,1)S(1)}, bf16[2,32,32,128]{3,2,1,0:T(8,128)(2,1)}, u32[]{:S(2)}, u32[]{:S(2)}) %collective-permute-start.2) | collective-permute-done | bytes 524320 | tf_op jit(solution)/shard_map/ppermute | solution.py:18
  53.9 1.5 collective-permute-start.7
  55.4 1.9 constant_dynamic-update-slice_fusion.5
  57.3 0.0 collective-permute-done.3
  57.3 1.9 constant_dynamic-update-slice_fusion.4
  59.2 42.6 %collective-permute-done.4 = bf16[2,32,32,128]{3,2,1,0:T(8,128)(2,1)S(1)} collective-permute-done((bf16[2,32,32,128]{3,2,1,0:T(8,128)(2,1)S(1)}, bf16[2,32,32,128]{3,2,1,0:T(8,128)(2,1)S(1)}, u32[]{:S(2)}, u32[]{:S(2)}) %collective-permute-start.4) | collective-permute-done | bytes 524320 | tf_op jit(solution)/shard_map/ppermute | solution.py:18
  101.8 0.9 constant_dynamic-update-slice_fusion.3
  102.7 3.5 collective-permute-done.5
  106.2 0.9 constant_dynamic-update-slice_fusion.2
  107.1 2.6 collective-permute-done.6
  109.7 0.9 constant_dynamic-update-slice_fusion.1
  110.6 3.3 collective-permute-done.7
  113.9 0.9 constant_dynamic-update-slice_fusion
  114.8 17.3 %copy.18 = bf16[64,32,1152]{0,1,2:T(8,128)(2,1)} copy(bf16[64,32,1152]{2,1,0:T(8,128)(2,1)} %bitcast.45) | data formatting | bytes 9437184 | tf_op jit(solution)/shard_map/reshape | solution.py:39
  132.1 7.0 %gather_fusion = bf16[512,64,32]{1,2,0:T(8,128)(2,1)} fusion(bf16[64,32,1152]{0,1,2:T(8,128)(2,1)} %copy.18, s32[1024]{0:T(1024)S(1)} %pad_clamp_fusion), kind=kCustom, calls=%fused_computation | custom fusion | bytes 4196352 | tf_op jit(solution)/shard_map/jit(_take)/gather | solution.py:42
  139.1 3.2 select_bitcast_fusion
  142.3 8.3 %multiply_convert_fusion = bf16[32,256,512]{2,1,0:T(8,128)(2,1)} fusion(bf16[64,32,256]{2,0,1:T(8,128)(2,1)S(1)} %reshape.207, bf16[64,32,512]{0,1,2:T(8,128)(2,1)S(1)} %select_bitcast_fusion), kind=kOutput, calls=%fused_computation.2 | convolution fusion | flops 545259520 | bytes 11534336 | tf_op jit(solution)/shard_map/wfbi,wfbj->fbij/dot_general | solution.py:52
  150.6 12.6 %reshape.209 = bf16[32,1,2,128,4,128]{5,4,3,2,0,1:T(4,128)(2,1)} reshape(bf16[32,256,512]{2,1,0:T(8,128)(2,1)} %multiply_convert_fusion) | data formatting | bytes 16777216 | tf_op jit(solution)/shard_map/reshape | solution.py:56
  163.1 9.1 %copy.20 = bf16[32,2,1,4,128,128]{5,4,3,0,1,2:T(8,128)(2,1)} copy(bf16[32,2,1,4,128,128]{5,3,4,1,0,2:T(4,128)(2,1)} %bitcast.44) | data formatting | bytes 16777216 | tf_op jit(solution)/shard_map/transpose | solution.py:56
  172.2 10.4 %reshape_reshape.3 = bf16[32,2,65536]{2,0,1:T(8,128)(2,1)} reshape(bf16[32,2,1,4,128,128]{5,4,3,0,1,2:T(8,128)(2,1)} %copy.20) | data formatting | bytes 16777216 | tf_op jit(solution)/shard_map/reshape;reshape | solution.py:63
  182.6 7.9 %convolution_bitcast_fusion = f32[32,65536]{1,0:T(8,128)} fusion(bf16[32,2,65536]{2,0,1:T(8,128)(2,1)} %reshape_reshape.3, bf16[32,1,32]{0,2,1:T(8,128)(2,1)S(1)} %get-tuple-element.10, bf16[32,1,32]{0,2,1:T(8,128)(2,1)S(1)} %get-tuple-element.9), kind=kOutput, calls=%fused_computation.1 | convolution fusion | flops 268437504 | bytes 16781312 | tf_op jit(solution)/shard_map/frl,frx->lx/dot_general | solution.py:65
  190.5 0.0 all-reduce.3.cloned.1.call-update
  190.6 0.6 copy-done
  191.2 0.6 dynamic-slice
  192.5 398.1 %all-reduce.3.cloned.1.call-done = f32[32,65536]{1,0:T(8,128)} async-done(((f32[32,65536]{1,0:T(8,128)}), f32[32,65536]{1,0:T(8,128)}) %all-reduce.3.cloned.1.call-update) | async-done | bytes 8388624
  590.6 1.9 fusion.2
  592.5 0.7 copy.22
  (7 shorter events, 0.1 us)
Async XLA Ops:
  6.5 584.1 %all-reduce.3.cloned.1.call-start = ((), (), s32[]{:S(2)}) async-start(), calls=%async_computation | async-start | bytes 16777216
  9.2 14.4 %collective-permute-start = (bf16[2,32,32,128]{3,2,1,0:T(8,128)(2,1)S(1)}, bf16[2,32,32,128]{3,2,1,0:T(8,128)(2,1)}, u32[]{:S(2)}, u32[]{:S(2)}) collective-permute-start(bf16[2,32,32,128]{3,2,1,0:T(8,128)(2,1)S(1)} %get-tuple-element.6), channel_id=1, source_target_pairs={{16,0},{32,16},{48,32},{64,48},{80,64},{96,80},{112,96},{128,112},... | collective-permute-start | bytes 1572872 | tf_op jit(solution)/shard_map/ppermute | solution.py:18
  11.8 24.8 %collective-permute-start.1 = (bf16[2,32,32,128]{3,2,1,0:T(8,128)(2,1)S(1)}, bf16[2,32,32,128]{3,2,1,0:T(8,128)(2,1)}, u32[]{:S(2)}, u32[]{:S(2)}) collective-permute-start(bf16[2,32,32,128]{3,2,1,0:T(8,128)(2,1)S(1)} %get-tuple-element.6), channel_id=1, source_target_pairs={{32,0},{48,16},{64,32},{80,48},{96,64},{112,80},{128,96},{144,112}... | collective-permute-start | bytes 1572872 | tf_op jit(solution)/shard_map/ppermute | solution.py:18
  15.6 38.2 %collective-permute-start.2 = (bf16[2,32,32,128]{3,2,1,0:T(8,128)(2,1)S(1)}, bf16[2,32,32,128]{3,2,1,0:T(8,128)(2,1)}, u32[]{:S(2)}, u32[]{:S(2)}) collective-permute-start(bf16[2,32,32,128]{3,2,1,0:T(8,128)(2,1)S(1)} %get-tuple-element.6), channel_id=1, source_target_pairs={{48,0},{64,16},{80,32},{96,48},{112,64},{128,80},{144,96},{160,112... | collective-permute-start | bytes 1572872 | tf_op jit(solution)/shard_map/ppermute | solution.py:18
  17.6 39.7 %collective-permute-start.3 = (bf16[2,32,32,128]{3,2,1,0:T(8,128)(2,1)S(1)}, bf16[2,32,32,128]{3,2,1,0:T(8,128)(2,1)}, u32[]{:S(2)}, u32[]{:S(2)}) collective-permute-start(bf16[2,32,32,128]{3,2,1,0:T(8,128)(2,1)S(1)} %get-tuple-element.6), channel_id=1, source_target_pairs={{64,0},{80,16},{96,32},{112,48},{128,64},{144,80},{160,96},{176,11... | collective-permute-start | bytes 1572872 | tf_op jit(solution)/shard_map/ppermute | solution.py:18
  18.9 82.9 %collective-permute-start.4 = (bf16[2,32,32,128]{3,2,1,0:T(8,128)(2,1)S(1)}, bf16[2,32,32,128]{3,2,1,0:T(8,128)(2,1)S(1)}, u32[]{:S(2)}, u32[]{:S(2)}) collective-permute-start(bf16[2,32,32,128]{3,2,1,0:T(8,128)(2,1)S(1)} %get-tuple-element.6), channel_id=1, source_target_pairs={{80,0},{96,16},{112,32},{128,48},{144,64},{160,80},{176,96},{192,1... | collective-permute-start | bytes 1572872 | tf_op jit(solution)/shard_map/ppermute | solution.py:18
  23.6 82.6 %collective-permute-start.5 = (bf16[2,32,32,128]{3,2,1,0:T(8,128)(2,1)S(1)}, bf16[2,32,32,128]{3,2,1,0:T(8,128)(2,1)S(1)}, u32[]{:S(2)}, u32[]{:S(2)}) collective-permute-start(bf16[2,32,32,128]{3,2,1,0:T(8,128)(2,1)S(1)} %get-tuple-element.6), channel_id=1, source_target_pairs={{96,0},{112,16},{128,32},{144,48},{160,64},{176,80},{192,96},{208,... | collective-permute-start | bytes 1572872 | tf_op jit(solution)/shard_map/ppermute | solution.py:18
  36.6 73.1 %collective-permute-start.6 = (bf16[2,32,32,128]{3,2,1,0:T(8,128)(2,1)S(1)}, bf16[2,32,32,128]{3,2,1,0:T(8,128)(2,1)S(1)}, u32[]{:S(2)}, u32[]{:S(2)}) collective-permute-start(bf16[2,32,32,128]{3,2,1,0:T(8,128)(2,1)S(1)} %get-tuple-element.6), channel_id=1, source_target_pairs={{112,0},{128,16},{144,32},{160,48},{176,64},{192,80},{208,96},{224... | collective-permute-start | bytes 1572872 | tf_op jit(solution)/shard_map/ppermute | solution.py:18
  53.9 60.0 %collective-permute-start.7 = (bf16[2,32,32,128]{3,2,1,0:T(8,128)(2,1)S(1)}, bf16[2,32,32,128]{3,2,1,0:T(8,128)(2,1)S(1)}, u32[]{:S(2)}, u32[]{:S(2)}) collective-permute-start(bf16[2,32,32,128]{3,2,1,0:T(8,128)(2,1)S(1)} %get-tuple-element.6), channel_id=1, source_target_pairs={{128,0},{144,16},{160,32},{176,48},{192,64},{208,80},{224,96},{240... | collective-permute-start | bytes 1572872 | tf_op jit(solution)/shard_map/ppermute | solution.py:18
  190.5 0.7 copy-start
Sparse Core Ops, SparseCore 0:
  190.7 399.8 all-reduce.2
where the time goes:
time: 602 us; the launch traced here: 600 us
  waiting for transfers between devices  474 us (79%)
  local copies, waits for them, and re-layouts  71.3 us (12%)
  matrix products  16.2 us (3%)
  starting transfers between devices  14.9 us (2%)
  between operations  14.2 us (2%)
  other arithmetic  8.93 us (1%)
    unnamed x2, waiting for transfers between devices  398 us
    ppermute x8, waiting for transfers between devices, from_behind(): lax.ppermute(value, axis, [(source, source + steps) for source in range(i...  76.3 us
    reshape x1, local copies, waits for them, and re-layouts, on_device(): right_all = extended.reshape(2 * windows, bins_here, extended.shape[3])  17.3 us
    ppermute x8, starting transfers between devices, from_behind(): lax.ppermute(value, axis, [(source, source + steps) for source in range(i...  14.9 us
    reshape x1, local copies, waits for them, and re-layouts, on_device(): cross.reshape(bins_here, blocks_here, 2, BS, K, BS)  12.6 us
    unnamed x11, local copies, waits for them, and re-layouts  12.3 us
  transfers between devices with their start and end apart: 9, of which 8 were waited for; matrix products, arithmetic and copies ran while one was open for 2% of the time, Pallas kernels for 0%

commit v1 on v0

v1 whole, which is shorter than its diff:
```python
import math

import jax
import jax.numpy as jnp
import ml_dtypes
import numpy as np
from jax import lax
from jax.experimental import pallas as pl
from jax.experimental.pallas import tpu as pltpu
from jax.sharding import PartitionSpec as P

BS = 128
NF = 512
REACH = 8
K = 4
W = 32
LAGS = 32
BANDS = 16
BINS = NF // BANDS
DEPTH = 2 * W * BINS
HALF = W * BINS
CHUNKS = 4
CROWS = DEPTH // CHUNKS
TILE = 256
XROWS = LAGS // 4 * BS
ZROWS = LAGS // 16 * BS
SCALE = 1.0 / math.sqrt(W) / math.sqrt(NF)


def lag_table():
    bins = np.arange(NF)[:, None]
    lags = np.arange(LAGS)[None, :] - LAGS // 2
    angles = (bins * lags % (2 * NF)) * (math.pi / NF)
    table = np.stack([np.cos(angles), -np.sin(angles)], axis=2)
    table = table.astype(np.float32).astype(ml_dtypes.bfloat16).astype(np.float32)
    table = table.reshape(BANDS, BINS, 2 * LAGS).transpose(0, 2, 1)
    return np.tile(table, (1, 1, BS // BINS))


def kernel(
    spectra, mask, offsets, table, out,
    blocks, turned, left, right, sums, own, got, zsums, zown, zgot,
    gather_send, gather_recv, sib_send, x_send, x_recv, z_send, z_recv,
):
    fibre, band = lax.axis_index("fibre"), lax.axis_index("band")
    z_lo, y, core = fibre // 8, fibre // 2 % 4, fibre % 2
    chip = fibre // 2
    x, z_hi = band // 4, band % 4

    def at_fibre(zz, yy, cc):
        return {"fibre": (zz * 4 + yy) * 2 + cc, "band": band}

    def at_band(xx, zz):
        return {"fibre": fibre, "band": xx * 4 + zz}

    sibling = at_fibre(z_lo, y, 1 - core)
    barrier = pltpu.get_barrier_semaphore()
    peers = [sibling, at_fibre(1 - z_lo, y, core)]
    peers += [at_fibre(z_lo, (y + j) % 4, core) for j in (1, 2, 3)]
    peers += [at_band((x + j) % 4, z_hi) for j in (1, 2, 3)]
    peers += [at_band(x, (z_hi + j) % 4) for j in (1, 2, 3)]
    for peer in peers:
        pl.semaphore_signal(barrier, inc=1, device_id=peer, device_id_type=pl.DeviceIdType.MESH)

    alive = mask[...].astype(jnp.bfloat16)
    blocks[0] = spectra[...] * alive
    pl.semaphore_wait(barrier, len(peers))

    def remote(src, dst, send, recv, device):
        return pltpu.make_async_remote_copy(
            src_ref=src, dst_ref=dst, send_sem=send, recv_sem=recv,
            device_id=device, device_id_type=pl.DeviceIdType.MESH,
        )

    def rows_of(ch):
        return pl.ds(ch * CROWS, CROWS)

    def far(ch):
        return remote(
            blocks.at[0, rows_of(ch)], blocks.at[8, rows_of(ch)],
            gather_send.at[3, ch], gather_recv.at[8, ch], at_fibre(1 - z_lo, y, core),
        )

    def near(j, ch):
        src = jnp.where(y >= j, 0, 8)
        return remote(
            blocks.at[src, rows_of(ch)], blocks.at[2 * j, rows_of(ch)],
            gather_send.at[j - 1, ch], gather_recv.at[2 * j, ch], at_fibre(z_lo, (y - j + 4) % 4, core),
        )

    def across(j, ch):
        return remote(
            blocks.at[2 * j + 2 * (1 - core), rows_of(ch)], blocks.at[2 * j + 1, rows_of(ch)],
            sib_send.at[j, ch], gather_recv.at[2 * j + 1, ch], sibling,
        )

    across_here = [chip + j + (1 - core) <= 7 for j in range(4)]
    across_there = [chip + j + core <= 7 for j in range(4)]
    even_here = [chip + j <= 7 for j in range(5)]

    @pl.when(z_lo == 1)
    def _():
        for ch in range(CHUNKS):
            far(ch).start()

    for j in (1, 2, 3):
        @pl.when(y >= j)
        def _(j=j):
            for ch in range(CHUNKS):
                near(j, ch).start()

    @pl.when(core == 1)
    def _():
        for ch in range(CHUNKS):
            across(0, ch).start()

    for r in range(2):
        for g in range(HALF // BS):
            piece = blocks[0, pl.ds(r * HALF + g * BS, BS), :].astype(jnp.float32)
            turned[r, :, pl.ds(g * BS, BS)] = piece.T

    def build(lag, carry):
        t0 = table[pl.ds(2 * lag, 1), :]
        t1 = table[pl.ds(2 * lag + 1, 1), :]
        rows = pl.ds(pl.multiple_of(lag * BS, BS), BS)
        for g in range(HALF // BS):
            re = turned[0, :, pl.ds(g * BS, BS)]
            im = turned[1, :, pl.ds(g * BS, BS)]
            left[rows, pl.ds(g * BS, BS)] = (t0 * re + t1 * im).astype(jnp.bfloat16)
            left[rows, pl.ds(HALF + g * BS, BS)] = (t0 * im - t1 * re).astype(jnp.bfloat16)
        return carry

    for ch in range(CHUNKS):
        lax.fori_loop(ch * LAGS // CHUNKS, (ch + 1) * LAGS // CHUNKS, build, 0)

        @pl.when(z_lo == 0)
        def _(ch=ch):
            far(ch).wait_recv()
            for j in (1, 2, 3):
                @pl.when(y < j)
                def _(j=j):
                    near(j, ch).start()

            @pl.when(core == 0)
            def _():
                across(3, ch).start()

    def pass_on(j):
        @pl.when(even_here[j])
        def _():
            for ch in range(CHUNKS):
                near(j, ch).wait_recv()

        send_j = j - 1 + core

        @pl.when(jnp.logical_and(chip + j <= 7, send_j <= 3))
        def _():
            for ch in range(CHUNKS):
                across(send_j, ch).start()

    def gather_rest():
        for j in (1, 2, 3):
            pass_on(j)
        for j in range(4):
            @pl.when(across_there[j])
            def _(j=j):
                for ch in range(CHUNKS):
                    across(j, ch).wait_recv()

    def x_copy(k, dd):
        return remote(
            sums.at[k, dd - 1], got.at[k, dd - 1], x_send.at[k, dd - 1], x_recv.at[k, dd - 1],
            at_band((x + dd) % 4, z_hi),
        )

    def z_copy(k, ee):
        return remote(
            zsums.at[k, ee - 1], zgot.at[k, ee - 1], z_send.at[k, ee - 1], z_recv.at[k, ee - 1],
            at_band(x, (z_hi + ee) % 4),
        )

    def multiply(k):
        for dd in (2, 1, 3, 0):
            base = (x + dd) % 4 * XROWS

            def tile(t, carry, dd=dd, base=base):
                here = pl.ds(pl.multiple_of(t * TILE, TILE), TILE)
                rows = pl.ds(pl.multiple_of(base + t * TILE, TILE), TILE)
                total = jnp.dot(left[rows, :], right[...], preferred_element_type=jnp.float32)
                if dd == 0:
                    own[k, here, :] = total
                else:
                    sums[k, dd - 1, here, :] = total.astype(jnp.bfloat16)
                return carry

            lax.fori_loop(0, XROWS // TILE, tile, 0)
            if dd != 0:
                x_copy(k, dd).start()

    def reduce_x(k):
        for dd in (1, 3, 2):
            x_copy(k, dd).wait_recv()
        for ee in (2, 1, 3, 0):
            rows = pl.ds(pl.multiple_of((z_hi + ee) % 4 * ZROWS, ZROWS), ZROWS)
            total = own[k, rows, :]
            for s in range(3):
                total += got[k, s, rows, :].astype(jnp.float32)
            if ee == 0:
                zown[k] = total
            else:
                zsums[k, ee - 1] = total.astype(jnp.bfloat16)
                z_copy(k, ee).start()

    def finish(k):
        for ee in (1, 3, 2):
            z_copy(k, ee).wait_recv()
        total = zown[k]
        for s in range(3):
            total += zgot[k, s].astype(jnp.float32)
        done = (total * SCALE).astype(jnp.bfloat16)
        for lag in range(2):
            out[lag, 0, k] = done[lag * BS:(lag + 1) * BS]

    @pl.when(z_lo == 1)
    def _():
        gather_rest()

    right[...] = blocks[jnp.minimum(REACH, 15 - fibre)]
    multiply(0)

    @pl.when(z_lo == 0)
    def _():
        gather_rest()

    right[...] = blocks[offsets[0, 1]]
    multiply(1)
    reduce_x(0)
    right[...] = blocks[offsets[0, 2]]
    multiply(2)
    reduce_x(1)
    finish(0)
    right[...] = blocks[offsets[0, 3]]
    multiply(3)
    reduce_x(2)
    finish(1)
    reduce_x(3)
    finish(2)
    finish(3)

    @pl.when(z_lo == 1)
    def _():
        for ch in range(CHUNKS):
            far(ch).wait_send()

    for j in (1, 2, 3):
        @pl.when(jnp.logical_or(y >= j, z_lo == 0))
        def _(j=j):
            for ch in range(CHUNKS):
                near(j, ch).wait_send()

    for j in range(4):
        @pl.when(across_here[j])
        def _(j=j):
            for ch in range(CHUNKS):
                across(j, ch).wait_send()

    for k in range(K):
        for dd in (1, 2, 3):
            x_copy(k, dd).wait_send()
            z_copy(k, dd).wait_send()


def on_device(spectra, dead_mask, partner_offset):
    table = lax.dynamic_index_in_dim(jnp.asarray(lag_table()), lax.axis_index("band"), 0, False)
    vmem = pl.BlockSpec(memory_space=pltpu.VMEM)
    bf16, f32 = jnp.bfloat16, jnp.float32
    return pl.pallas_call(
        kernel,
        out_shape=jax.ShapeDtypeStruct((LAGS // BANDS, 1, K, BS, BS), bf16),
        in_specs=[vmem, vmem, pl.BlockSpec(memory_space=pltpu.SMEM), vmem],
        out_specs=vmem,
        scratch_shapes=[
            pltpu.VMEM((REACH + 1, DEPTH, BS), bf16),
            pltpu.VMEM((2, BS, HALF), f32),
            pltpu.VMEM((LAGS * BS, DEPTH), bf16),
            pltpu.VMEM((DEPTH, BS), bf16),
            pltpu.VMEM((K, 3, XROWS, BS), bf16),
            pltpu.VMEM((K, XROWS, BS), f32),
            pltpu.VMEM((K, 3, XROWS, BS), bf16),
            pltpu.VMEM((K, 3, ZROWS, BS), bf16),
            pltpu.VMEM((K, ZROWS, BS), f32),
            pltpu.VMEM((K, 3, ZROWS, BS), bf16),
            pltpu.SemaphoreType.DMA((4, CHUNKS)),
            pltpu.SemaphoreType.DMA((REACH + 1, CHUNKS)),
            pltpu.SemaphoreType.DMA((4, CHUNKS)),
            pltpu.SemaphoreType.DMA((K, 3)),
            pltpu.SemaphoreType.DMA((K, 3)),
            pltpu.SemaphoreType.DMA((K, 3)),
            pltpu.SemaphoreType.DMA((K, 3)),
        ],
        compiler_params=pltpu.CompilerParams(
            collective_id=0, has_side_effects=True, vmem_limit_bytes=56 * 1024 * 1024
        ),
        cost_estimate=pl.CostEstimate(
            flops=2 * LAGS * BS * DEPTH * K * BS, bytes_accessed=1 << 20, transcendentals=0
        ),
    )(spectra.reshape(DEPTH, BS), dead_mask.reshape(1, BS), partner_offset, table)


def solution(mesh):
    in_specs = (P(None, None, "band", "fibre"), P("fibre"), P("fibre", None))
    out_specs = P("band", "fibre", None, None, None)
    return jax.shard_map(
        on_device, mesh=mesh, in_specs=in_specs, out_specs=out_specs, check_vma=False
    )
```

time: 602 us -> 97.8 us (0.16)
  the two profiles are of different devices: /device:TPU:9 before, /device:TPU:33 now
where the time goes in v1:
time: 97.8 us; the launch traced here: 97.6 us
  Pallas kernels  94.5 us (97%)
  local copies, waits for them, and re-layouts  3.05 us (3%)
    pallas_call x1, Pallas kernels, on_device(): pl.pallas_call(kernel, out_shape=jax.ShapeDtypeStruct((LAGS // BANDS, 1,...  94.5 us

profile of v1, /device:TPU:33, one launch (start us, length us, event | category | flops | bytes accessed | tf_op | source)
XLA Modules:
  0.0 97.6 jit_solution(10987937611457727244)
XLA Ops:
  0.0 1.4 %dynamic-slice_bitcast_fusion.table = f32[64,128]{1,0:T(8,128)} fusion(f32[16,64,128]{2,1,0:T(8,128)} %constant.12.clone, s32[]{:T(128)S(6)} %select_n.4), kind=kLoop, calls=%fused_computation | loop fusion | bytes 65540 | tf_op jit(solution)/shard_map/jit(dynamic_index_in_dim)/squeeze | solution.py:274
  1.4 94.5 %shard_map.46 = bf16[2,1,4,128,128]{4,3,2,1,0:T(8,128)(2,1)} custom-call(bf16[2048,128]{1,0:T(8,128)(2,1)} %bitcast.4, s32[1,128]{1,0:T(1,128)} %bitcast.5, s32[1,4]{1,0:T(1,128)} %offsets.1, f32[64,128]{1,0:T(8,128)} %dynamic-slice_bitcast_fusion.table), custom_call_target="tpu_custom_call" | custom-call | flops 8589934592 | bytes 1048576 | tf_op jit(solution)/shard_map/pallas_call | solution.py:277
  95.9 1.7 %copy.6 = bf16[2,1,4,128,128]{4,3,2,1,0:T(8,128)(2,1)} copy(bf16[2,1,4,128,128]{4,3,2,1,0:T(8,128)(2,1)} %shard_map.46) | data formatting | bytes 524288

commit v2 on v1

v2 whole, which is shorter than its diff:
```python
import math

import jax
import jax.numpy as jnp
import ml_dtypes
import numpy as np
from jax import lax
from jax.experimental import pallas as pl
from jax.experimental.pallas import tpu as pltpu
from jax.sharding import PartitionSpec as P

BS = 128
NF = 512
REACH = 8
K = 4
W = 32
LAGS = 32
BANDS = 16
BINS = NF // BANDS
DEPTH = 2 * W * BINS
HALF = W * BINS
CHUNKS = 4
CROWS = DEPTH // CHUNKS
XROWS = LAGS // 4 * BS
HX = XROWS // 2
ZROWS = LAGS // 16 * BS
TAIL = 16
SCALE = 1.0 / math.sqrt(W) / math.sqrt(NF)


def lag_table():
    bins = np.arange(NF)[:, None]
    lags = np.arange(LAGS)[None, :] - LAGS // 2
    angles = (bins * lags % (2 * NF)) * (math.pi / NF)
    table = np.stack([np.cos(angles), -np.sin(angles)], axis=2)
    table = table.astype(np.float32).astype(ml_dtypes.bfloat16).astype(np.float32)
    table = table.reshape(BANDS, BINS, 2 * LAGS).transpose(0, 2, 1)
    return np.tile(table, (1, 1, BS // BINS))


def kernel(
    spectra, mask, offsets, tables, out,
    blocks, turned, left, right, table, part, go, come, zsums, zgot,
    table_sem, gather_send, relay_send, gather_recv, sib_send, x_send, x_recv, z_send, z_recv,
):
    fibre, band = lax.axis_index("fibre"), lax.axis_index("band")
    z_lo, y, core = fibre // 8, fibre // 2 % 4, fibre % 2
    chip = fibre // 2
    x, z_hi = band // 4, band % 4

    def at_fibre(zz, yy, cc):
        return {"fibre": (zz * 4 + yy) * 2 + cc, "band": band}

    def at_band(xx, zz):
        return {"fibre": fibre, "band": xx * 4 + zz}

    sibling = at_fibre(z_lo, y, 1 - core)
    other_z = at_fibre(1 - z_lo, y, core)
    y_down, y_up = at_fibre(z_lo, (y + 3) % 4, core), at_fibre(z_lo, (y + 1) % 4, core)
    x_down, x_up = at_band((x + 3) % 4, z_hi), at_band((x + 1) % 4, z_hi)
    barrier = pltpu.get_barrier_semaphore()
    peers = [sibling, other_z, y_down, y_up, x_down, x_up]
    peers += [at_band(x, (z_hi + j) % 4) for j in (1, 2, 3)]
    for peer in peers:
        pl.semaphore_signal(barrier, inc=1, device_id=peer, device_id_type=pl.DeviceIdType.MESH)

    table_copy = pltpu.make_async_copy(tables.at[band], table, table_sem)
    table_copy.start()
    alive = mask[...].astype(jnp.bfloat16)
    blocks[0] = spectra[...] * alive
    pl.semaphore_wait(barrier, len(peers))

    def remote(src, dst, send, recv, device):
        return pltpu.make_async_remote_copy(
            src_ref=src, dst_ref=dst, send_sem=send, recv_sem=recv,
            device_id=device, device_id_type=pl.DeviceIdType.MESH,
        )

    def rows_of(ch):
        return pl.ds(ch * CROWS, CROWS)

    def far(ch):
        return remote(
            blocks.at[0, rows_of(ch)], blocks.at[8, rows_of(ch)],
            gather_send.at[0, ch], gather_recv.at[8, ch], other_z,
        )

    def near(j, ch):
        src = jnp.where(y >= j, 0, 8)
        return remote(
            blocks.at[src, rows_of(ch)], blocks.at[2 * j, rows_of(ch)],
            gather_send.at[j, ch], gather_recv.at[2 * j, ch], y_down if j == 1 else y_up,
        )

    def relay(j, ch):
        return remote(
            blocks.at[2 * j, rows_of(ch)], blocks.at[4, rows_of(ch)],
            relay_send.at[j // 2, ch], gather_recv.at[4, ch], y_down if j == 1 else y_up,
        )

    def across(j, ch):
        return remote(
            blocks.at[2 * j + 2 * (1 - core), rows_of(ch)], blocks.at[2 * j + 1, rows_of(ch)],
            sib_send.at[j, ch], gather_recv.at[2 * j + 1, ch], sibling,
        )

    def relays(j, ch):
        first = ch < CHUNKS // 2
        if j == 1:
            goes = jnp.logical_or(y == 1, y >= 2) if first else y == 1
        else:
            goes = y == 2 if first else y <= 2
        return jnp.logical_and(chip + j <= 7, goes)

    def near_goes(j):
        return jnp.logical_or(y >= j, jnp.logical_and(z_lo == 0, y != 3))

    @pl.when(z_lo == 1)
    def _():
        for ch in range(CHUNKS):
            far(ch).start()

    for j in (1, 3):
        @pl.when(y >= j)
        def _(j=j):
            for ch in range(CHUNKS):
                near(j, ch).start()

    @pl.when(core == 1)
    def _():
        for ch in range(CHUNKS):
            across(0, ch).start()

    def take_far(ch):
        far(ch).wait_recv()
        for j in (1, 3):
            @pl.when(y < j if j == 1 else y < 3)
            def _(j=j):
                near(j, ch).start()

        @pl.when(core == 0)
        def _():
            across(3, ch).start()

    def take(j, ch):
        @pl.when(chip + j <= 7)
        def _():
            remote(
                blocks.at[0, rows_of(ch)], blocks.at[2 * j, rows_of(ch)],
                gather_send.at[0, ch], gather_recv.at[2 * j, ch], y_up,
            ).wait_recv()
            if j != 2:
                @pl.when(relays(j, ch))
                def _():
                    relay(j, ch).start()
            across(j - 1 + core, ch).start()

    def build(lag, carry):
        t0 = table[pl.ds(2 * lag, 1), :]
        t1 = table[pl.ds(2 * lag + 1, 1), :]
        rows = pl.ds(pl.multiple_of(lag * BS, BS), BS)
        for g in range(HALF // BS):
            re = turned[0, :, pl.ds(g * BS, BS)]
            im = turned[1, :, pl.ds(g * BS, BS)]
            left[rows, pl.ds(g * BS, BS)] = (t0 * re + t1 * im).astype(jnp.bfloat16)
            left[rows, pl.ds(HALF + g * BS, BS)] = (t0 * im - t1 * re).astype(jnp.bfloat16)
        return carry

    def turn(g, carry):
        rows = pl.ds(pl.multiple_of(g * BS, BS), BS)
        for r in range(2):
            turned[r, :, rows] = blocks[0, pl.ds(pl.multiple_of(r * HALF + g * BS, BS), BS), :].astype(jnp.float32).T
        return carry

    lax.fori_loop(0, HALF // BS, turn, 0)
    table_copy.wait()
    lax.fori_loop(0, LAGS // 2, build, 0)

    def step(s):
        if s < CHUNKS:
            @pl.when(z_lo == 0)
            def _():
                take_far(s)
            take(1, s)
        if 1 <= s <= CHUNKS:
            take(3, s - 1)
        if 2 <= s:
            take(2, s - 2)

    for s in range(CHUNKS):
        step(s)
        lax.fori_loop(LAGS // 2 + s * LAGS // 8, LAGS // 2 + (s + 1) * LAGS // 8, build, 0)

    def siblings_done():
        for j in range(4):
            @pl.when(chip + j + core <= 7)
            def _(j=j):
                for ch in range(CHUNKS):
                    across(j, ch).wait_recv()

    def middle(k, way):
        return remote(
            go.at[k, way, 0], come.at[k, way, 0], x_send.at[k, way, 0], x_recv.at[k, way, 0],
            x_down if way else x_up,
        )

    def straight(k, way):
        return remote(
            go.at[k, way, 1], come.at[k, way, 1], x_send.at[k, way, 1], x_recv.at[k, way, 1],
            x_down if way else x_up,
        )

    def summed(k, way):
        return remote(
            go.at[k, way, 2], come.at[k, way, 2], x_send.at[k, way, 2], x_recv.at[k, way, 2],
            x_down if way else x_up,
        )

    def z_copy(k, ee):
        return remote(
            zsums.at[k, ee - 1], zgot.at[k, ee - 1], z_send.at[k, ee - 1], z_recv.at[k, ee - 1],
            at_band(x, (z_hi + ee) % 4),
        )

    square = (BS, BS)
    diagonal = lax.broadcasted_iota(jnp.int32, square, 0) == lax.broadcasted_iota(jnp.int32, square, 1)
    tail_row = lax.broadcasted_iota(jnp.int32, (TAIL, BS), 0)

    def pack(message, lags, value_of):
        tail = jnp.zeros((TAIL, BS), jnp.float32)
        for lag in range(lags):
            value = value_of(lag)
            rounded = value.astype(jnp.bfloat16)
            message[pl.ds(lag * BS, BS), :] = rounded
            rest = jnp.where(diagonal, value - rounded.astype(jnp.float32), 0.0)
            tail = jnp.where(tail_row == lag, jnp.sum(rest, axis=0, keepdims=True), tail)
        message[pl.ds(lags * BS, TAIL), :] = tail.astype(jnp.bfloat16)

    def unpack(message, lags, lag):
        tail = message[pl.ds(lags * BS, TAIL), :].astype(jnp.float32)[lag:lag + 1]
        return message[pl.ds(lag * BS, BS), :].astype(jnp.float32) + jnp.where(diagonal, tail, 0.0)

    def part_of(k, q, lag):
        return part[k, q, pl.ds(lag * BS, BS), :]

    def multiply(k, between=None):
        def quarter(q, carry):
            @pl.when(q == 3)
            def _():
                for way in (0, 1):
                    middle(k, way).wait_recv()
                    def both(lag, way=way):
                        return part_of(k, 1 + way, way * 4 + lag) + unpack(come.at[k, way, 0], 4, lag)

                    pack(go.at[k, way, 2], 4, both)
                    summed(k, way).start()

            ahead = jnp.where(q == 0, 2, jnp.where(q == 1, 1, jnp.where(q == 2, 3, 0)))
            rows = pl.ds(pl.multiple_of((x + ahead) % 4 * XROWS, XROWS), XROWS)
            part[k, q] = jnp.dot(left[rows, :], right[...], preferred_element_type=jnp.float32)

            @pl.when(q == 0)
            def _():
                for way in (0, 1):
                    pack(go.at[k, way, 0], 4, lambda lag, way=way: part_of(k, 0, way * 4 + lag))
                    middle(k, way).start()

            for way in (0, 1):
                @pl.when(q == 1 + way)
                def _(way=way):
                    pack(go.at[k, way, 1], 4, lambda lag: part_of(k, 1 + way, (1 - way) * 4 + lag))
                    straight(k, way).start()

            if between is not None:
                between(q)
            return carry

        lax.fori_loop(0, 4, quarter, 0)

    def reduce_x(k):
        for way in (0, 1):
            straight(k, way).wait_recv()
            summed(k, way).wait_recv()
        for lag in range(8):
            up = 2 if lag < 4 else 1
            total = part_of(k, 3, lag) + unpack(come.at[k, 0, up], 4, lag % 4)
            part[k, 3, pl.ds(lag * BS, BS), :] = total + unpack(come.at[k, 1, 3 - up], 4, lag % 4)
        for ee in (2, 1, 3):
            def to_send(lag, ee=ee):
                row = ((z_hi + ee) % 4 * 2 + lag) * BS
                return part[k, 3, pl.ds(pl.multiple_of(row, BS), BS), :]

            pack(zsums.at[k, ee - 1], 2, to_send)
            z_copy(k, ee).start()

    def finish(k):
        for ee in (1, 3, 2):
            z_copy(k, ee).wait_recv()
        for lag in range(2):
            total = part[k, 3, pl.ds(pl.multiple_of((z_hi * 2 + lag) * BS, BS), BS), :]
            for s in range(3):
                total += unpack(zgot.at[k, s], 2, lag)
            out[lag, 0, k] = (total * SCALE).astype(jnp.bfloat16)

    @pl.when(z_lo == 1)
    def _():
        step(CHUNKS)
        step(CHUNKS + 1)
        siblings_done()

    def between(q):
        for s in (0, 1):
            @pl.when(jnp.logical_and(z_lo == 0, q == s))
            def _(s=s):
                step(CHUNKS + s)

    right[...] = blocks[jnp.minimum(REACH, 15 - fibre)]
    multiply(0, between)

    @pl.when(z_lo == 0)
    def _():
        siblings_done()

    right[...] = blocks[offsets[0, 1]]
    multiply(1)
    reduce_x(0)
    right[...] = blocks[offsets[0, 2]]
    multiply(2)
    reduce_x(1)
    finish(0)
    right[...] = blocks[offsets[0, 3]]
    multiply(3)
    reduce_x(2)
    finish(1)
    reduce_x(3)
    finish(2)
    finish(3)

    @pl.when(z_lo == 1)
    def _():
        for ch in range(CHUNKS):
            far(ch).wait_send()

    for j in (1, 3):
        @pl.when(near_goes(j))
        def _(j=j):
            for ch in range(CHUNKS):
                near(j, ch).wait_send()
        for ch in range(CHUNKS):
            @pl.when(relays(j, ch))
            def _(j=j, ch=ch):
                relay(j, ch).wait_send()

    for j in range(4):
        @pl.when(chip + j + (1 - core) <= 7)
        def _(j=j):
            for ch in range(CHUNKS):
                across(j, ch).wait_send()

    for k in range(K):
        for way in (0, 1):
            middle(k, way).wait_send()
            straight(k, way).wait_send()
            summed(k, way).wait_send()
        for ee in (1, 2, 3):
            z_copy(k, ee).wait_send()


def on_device(spectra, dead_mask, partner_offset):
    vmem = pl.BlockSpec(memory_space=pltpu.VMEM)
    bf16, f32 = jnp.bfloat16, jnp.float32
    return pl.pallas_call(
        kernel,
        out_shape=jax.ShapeDtypeStruct((LAGS // BANDS, 1, K, BS, BS), bf16),
        in_specs=[vmem, vmem, pl.BlockSpec(memory_space=pltpu.SMEM), pl.BlockSpec(memory_space=pl.ANY)],
        out_specs=vmem,
        scratch_shapes=[
            pltpu.VMEM((REACH + 1, DEPTH, BS), bf16),
            pltpu.VMEM((2, BS, HALF), f32),
            pltpu.VMEM((LAGS * BS, DEPTH), bf16),
            pltpu.VMEM((DEPTH, BS), bf16),
            pltpu.VMEM((2 * LAGS, BS), f32),
            pltpu.VMEM((K, 4, XROWS, BS), f32),
            pltpu.VMEM((K, 2, 3, HX + TAIL, BS), bf16),
            pltpu.VMEM((K, 2, 3, HX + TAIL, BS), bf16),
            pltpu.VMEM((K, 3, ZROWS + TAIL, BS), bf16),
            pltpu.VMEM((K, 3, ZROWS + TAIL, BS), bf16),
            pltpu.SemaphoreType.DMA,
            pltpu.SemaphoreType.DMA((4, CHUNKS)),
            pltpu.SemaphoreType.DMA((2, CHUNKS)),
            pltpu.SemaphoreType.DMA((REACH + 1, CHUNKS)),
            pltpu.SemaphoreType.DMA((4, CHUNKS)),
            pltpu.SemaphoreType.DMA((K, 2, 3)),
            pltpu.SemaphoreType.DMA((K, 2, 3)),
            pltpu.SemaphoreType.DMA((K, 3)),
            pltpu.SemaphoreType.DMA((K, 3)),
        ],
        compiler_params=pltpu.CompilerParams(
            collective_id=0, has_side_effects=True, vmem_limit_bytes=56 * 1024 * 1024
        ),
        cost_estimate=pl.CostEstimate(
            flops=2 * LAGS * BS * DEPTH * K * BS, bytes_accessed=1 << 20, transcendentals=0
        ),
    )(spectra.reshape(DEPTH, BS), dead_mask.reshape(1, BS), partner_offset, jnp.asarray(lag_table()))


def solution(mesh):
    in_specs = (P(None, None, "band", "fibre"), P("fibre"), P("fibre", None))
    out_specs = P("band", "fibre", None, None, None)
    return jax.shard_map(
        on_device, mesh=mesh, in_specs=in_specs, out_specs=out_specs, check_vma=False
    )
```

time: 97.8 us -> 84.2 us (0.86)
  the two profiles are of different devices: /device:TPU:33 before, /device:TPU:6 now
where the time goes in v2:
time: 84.2 us; the launch traced here: 84.1 us
  Pallas kernels  82.4 us (98%)
  local copies, waits for them, and re-layouts  1.67 us (2%)
    pallas_call x1, Pallas kernels, on_device(): pl.pallas_call(kernel, out_shape=jax.ShapeDtypeStruct((LAGS // BANDS, 1,...  82.4 us

profile of v2, /device:TPU:6, one launch (start us, length us, event | category | flops | bytes accessed | tf_op | source)
XLA Modules:
  0.0 84.1 jit_solution(17958424508753616960)
XLA Ops:
  0.0 82.4 %shard_map.46 = bf16[2,1,4,128,128]{4,3,2,1,0:T(8,128)(2,1)} custom-call(bf16[2048,128]{1,0:T(8,128)(2,1)} %bitcast.2, s32[1,128]{1,0:T(1,128)} %bitcast.3, s32[1,4]{1,0:T(1,128)} %offsets.1, f32[16,64,128]{2,1,0:T(8,128)} %constant.2.clone.tables), custom_call_target="tpu_custom_call" | custom-call | flops 8589934592 | bytes 1048576 | tf_op jit(solution)/shard_map/pallas_call | solution.py:372
  82.4 1.7 %copy.6 = bf16[2,1,4,128,128]{4,3,2,1,0:T(8,128)(2,1)} copy(bf16[2,1,4,128,128]{4,3,2,1,0:T(8,128)(2,1)} %shard_map.46) | data formatting | bytes 524288

commit v3 on v2

--- a/solution.py
+++ b/solution.py
@@ -40,8 +40,8 @@
 
 def kernel(
     spectra, mask, offsets, tables, out,
-    blocks, turned, left, right, table, part, go, come, zsums, zgot,
-    table_sem, gather_send, relay_send, gather_recv, sib_send, x_send, x_recv, z_send, z_recv,
+    blocks, spare, turned, left, right, table, part, go, come, zsums, zgot,
+    table_sem, gather_send, relay_send, aside_send, around_send, around_recv, gather_recv, sib_send, x_send, x_recv, z_send, z_recv,
 ):
     fibre, band = lax.axis_index("fibre"), lax.axis_index("band")
     z_lo, y, core = fibre // 8, fibre // 2 % 4, fibre % 2
@@ -104,16 +104,38 @@
             sib_send.at[j, ch], gather_recv.at[2 * j + 1, ch], sibling,
         )
 
+    def aside(ch):
+        return remote(
+            blocks.at[0, rows_of(ch)], blocks.at[8, rows_of(ch)],
+            aside_send.at[ch], gather_recv.at[8, ch], y_up,
+        )
+
+    def aside_on(ch):
+        return remote(
+            blocks.at[8, rows_of(ch)], blocks.at[6, rows_of(ch)],
+            aside_send.at[ch], gather_recv.at[6, ch], other_z,
+        )
+
+    upper = range(CHUNKS // 2, CHUNKS)
+    last_rows = rows_of(CHUNKS - 1)
+
+    def around():
+        return remote(blocks.at[0, last_rows], spare, around_send, around_recv, y_up)
+
+    def around_on():
+        return remote(spare, blocks.at[4, last_rows], around_send, gather_recv.at[4, CHUNKS - 1], y_up)
+
     def relays(j, ch):
         first = ch < CHUNKS // 2
         if j == 1:
-            goes = jnp.logical_or(y == 1, y >= 2) if first else y == 1
+            goes = y >= 1 if first else jnp.logical_and(y == 1, ch < CHUNKS - 1)
         else:
             goes = y == 2 if first else y <= 2
         return jnp.logical_and(chip + j <= 7, goes)
 
-    def near_goes(j):
-        return jnp.logical_or(y >= j, jnp.logical_and(z_lo == 0, y != 3))
+    def near_goes(j, ch):
+        limit = 1 if j == 1 else 2 if ch in upper else 3
+        return jnp.logical_or(y >= j, jnp.logical_and(z_lo == 0, y < limit))
 
     @pl.when(z_lo == 1)
     def _():
@@ -126,15 +148,24 @@
             for ch in range(CHUNKS):
                 near(j, ch).start()
 
+    @pl.when(y == 2)
+    def _():
+        around().start()
+
     @pl.when(core == 1)
     def _():
         for ch in range(CHUNKS):
             across(0, ch).start()
+
+    @pl.when(jnp.logical_and(z_lo == 1, y == 2))
+    def _():
+        for ch in upper:
+            aside(ch).start()
 
     def take_far(ch):
         far(ch).wait_recv()
         for j in (1, 3):
-            @pl.when(y < j if j == 1 else y < 3)
+            @pl.when(jnp.logical_and(y < j, near_goes(j, ch)))
             def _(j=j):
                 near(j, ch).start()
 
@@ -142,8 +173,8 @@
         def _():
             across(3, ch).start()
 
-    def take(j, ch):
-        @pl.when(chip + j <= 7)
+    def take(j, ch, when):
+        @pl.when(jnp.logical_and(chip + j <= 7, when))
         def _():
             remote(
                 blocks.at[0, rows_of(ch)], blocks.at[2 * j, rows_of(ch)],
@@ -155,6 +186,12 @@
                     relay(j, ch).start()
             across(j - 1 + core, ch).start()
 
+    def early(j, ch):
+        if j == 2:
+            return jnp.logical_and(z_lo == 1, y == 1)
+        last = jnp.logical_or(y == 1, y == 2) if j == 1 else y == 0
+        return jnp.where(z_lo == 0, relays(j, ch), last)
+
     def build(lag, carry):
         t0 = table[pl.ds(2 * lag, 1), :]
         t1 = table[pl.ds(2 * lag + 1, 1), :]
@@ -176,27 +213,53 @@
     table_copy.wait()
     lax.fori_loop(0, LAGS // 2, build, 0)
 
-    def step(s):
-        if s < CHUNKS:
-            @pl.when(z_lo == 0)
-            def _():
-                take_far(s)
-            take(1, s)
-        if 1 <= s <= CHUNKS:
-            take(3, s - 1)
-        if 2 <= s:
-            take(2, s - 2)
+    @pl.when(y == 3)
+    def _():
+        around().wait_recv()
+        around_on().start()
 
     for s in range(CHUNKS):
-        step(s)
+        @pl.when(z_lo == 0)
+        def _(s=s):
+            take_far(s)
+        take(1, s, early(1, s))
+        if s > 0:
+            take(3, s - 1, jnp.logical_and(early(3, s - 1), y != 1))
         lax.fori_loop(LAGS // 2 + s * LAGS // 8, LAGS // 2 + (s + 1) * LAGS // 8, build, 0)
 
-    def siblings_done():
+    def sibling_done(j):
+        for ch in range(CHUNKS):
+            across(j, ch).wait_recv()
+
+    @pl.when(z_lo == 1)
+    def _():
+        take(3, CHUNKS - 1, early(3, CHUNKS - 1))
+        for ch in range(CHUNKS):
+            take(2, ch, early(2, ch))
         for j in range(4):
-            @pl.when(chip + j + core <= 7)
+            @pl.when(jnp.logical_and(core == 0, y == 3 - j))
             def _(j=j):
-                for ch in range(CHUNKS):
-                    across(j, ch).wait_recv()
+                sibling_done(j)
+
+    def pass_on(ch, here):
+        take(3, ch, jnp.logical_and(z_lo == 0, jnp.logical_and(relays(3, ch), here)))
+
+    def gather_rest():
+        @pl.when(jnp.logical_and(z_lo == 1, y == 3))
+        def _():
+            for ch in upper:
+                aside(ch).wait_recv()
+                aside_on(ch).start()
+
+        for j in (1, 3, 2):
+            for ch in range(CHUNKS):
+                take(j, ch, jnp.logical_not(early(j, ch)))
+        for j in range(4):
+            taken = jnp.logical_and(z_lo == 1, jnp.logical_and(core == 0, y == 3 - j))
+
+            @pl.when(jnp.logical_and(chip + j + core <= 7, jnp.logical_not(taken)))
+            def _(j=j):
+                sibling_done(j)
 
     def middle(k, way):
         return remote(
@@ -243,36 +306,35 @@
     def part_of(k, q, lag):
         return part[k, q, pl.ds(lag * BS, BS), :]
 
-    def multiply(k, between=None):
+    def send_middle(k):
+        for way in (0, 1):
+            pack(go.at[k, way, 0], 4, lambda lag, way=way: part_of(k, 0, way * 4 + lag))
+            middle(k, way).start()
+
+    def send_straight(k, way):
+        pack(go.at[k, way, 1], 4, lambda lag: part_of(k, 1 + way, (1 - way) * 4 + lag))
+        straight(k, way).start()
+
+    def send_summed(k):
+        for way in (0, 1):
+            def both(lag, way=way):
+                return part_of(k, 1 + way, way * 4 + lag) + unpack(come.at[k, way, 0], 4, lag)
+
+            middle(k, way).wait_recv()
+            pack(go.at[k, way, 2], 4, both)
+            summed(k, way).start()
+
+    def multiply(slots, *after):
+        width = len(slots) * BS
+
         def quarter(q, carry):
-            @pl.when(q == 3)
-            def _():
-                for way in (0, 1):
-                    middle(k, way).wait_recv()
-                    def both(lag, way=way):
-                        return part_of(k, 1 + way, way * 4 + lag) + unpack(come.at[k, way, 0], 4, lag)
-
-                    pack(go.at[k, way, 2], 4, both)
-                    summed(k, way).start()
-
             ahead = jnp.where(q == 0, 2, jnp.where(q == 1, 1, jnp.where(q == 2, 3, 0)))
             rows = pl.ds(pl.multiple_of((x + ahead) % 4 * XROWS, XROWS), XROWS)
-            part[k, q] = jnp.dot(left[rows, :], right[...], preferred_element_type=jnp.float32)
-
-            @pl.when(q == 0)
-            def _():
-                for way in (0, 1):
-                    pack(go.at[k, way, 0], 4, lambda lag, way=way: part_of(k, 0, way * 4 + lag))
-                    middle(k, way).start()
-
-            for way in (0, 1):
-                @pl.when(q == 1 + way)
-                def _(way=way):
-                    pack(go.at[k, way, 1], 4, lambda lag: part_of(k, 1 + way, (1 - way) * 4 + lag))
-                    straight(k, way).start()
-
-            if between is not None:
-                between(q)
+            total = jnp.dot(left[rows, :], right[:, pl.ds(0, width)], preferred_element_type=jnp.float32)
+            for n, k in enumerate(slots):
+                part[k, q] = total[:, n * BS:(n + 1) * BS]
+            for at, then in enumerate(after):
+                pl.when(q == at)(then)
             return carry
 
         lax.fori_loop(0, 4, quarter, 0)
@@ -302,51 +364,67 @@
                 total += unpack(zgot.at[k, s], 2, lag)
             out[lag, 0, k] = (total * SCALE).astype(jnp.bfloat16)
 
-    @pl.when(z_lo == 1)
-    def _():
-        step(CHUNKS)
-        step(CHUNKS + 1)
-        siblings_done()
-
-    def between(q):
-        for s in (0, 1):
-            @pl.when(jnp.logical_and(z_lo == 0, q == s))
-            def _(s=s):
-                step(CHUNKS + s)
-
-    right[...] = blocks[jnp.minimum(REACH, 15 - fibre)]
-    multiply(0, between)
-
-    @pl.when(z_lo == 0)
-    def _():
-        siblings_done()
-
-    right[...] = blocks[offsets[0, 1]]
-    multiply(1)
-    reduce_x(0)
-    right[...] = blocks[offsets[0, 2]]
-    multiply(2)
-    reduce_x(1)
-    finish(0)
-    right[...] = blocks[offsets[0, 3]]
-    multiply(3)
+    right[:, pl.ds(0, BS)] = blocks[jnp.minimum(REACH, 15 - fibre)]
+    def zero_0():
+        send_middle(0)
+        pass_on(3, y != 1)
+        pass_on(2, y == 1)
+
+    def zero_1():
+        send_straight(0, 0)
+        pass_on(3, y == 1)
+
+    multiply((0,), zero_0, zero_1, lambda: send_straight(0, 1), lambda: send_summed(0))
+    gather_rest()
+    for n, slot in enumerate((1, 2)):
+        right[:, pl.ds(n * BS, BS)] = blocks[offsets[0, slot]]
+
+    def two_3():
+        send_middle(2)
+        send_summed(1)
+        send_straight(2, 0)
+        send_straight(2, 1)
+        reduce_x(0)
+
+    multiply((1, 2), lambda: send_middle(1), lambda: send_straight(1, 0), lambda: send_straight(1, 1), two_3)
+    right[:, pl.ds(0, BS)] = blocks[offsets[0, 3]]
+
+    def three_0():
+        send_middle(3)
+        send_summed(2)
+
+    def three_3():
+        finish(0)
+        reduce_x(1)
+        send_summed(3)
+
+    multiply((3,), three_0, lambda: send_straight(3, 0), lambda: send_straight(3, 1), three_3)
     reduce_x(2)
     finish(1)
     reduce_x(3)
     finish(2)
     finish(3)
 
+    @pl.when(y >= 2)
+    def _():
+        around().wait_send()
+
+    @pl.when(jnp.logical_and(z_lo == 1, y >= 2))
+    def _():
+        for ch in upper:
+            aside(ch).wait_send()
+
     @pl.when(z_lo == 1)
     def _():
         for ch in range(CHUNKS):
             far(ch).wait_send()
 
     for j in (1, 3):
-        @pl.when(near_goes(j))
-        def _(j=j):
-            for ch in range(CHUNKS):
+        for ch in range(CHUNKS):
+            @pl.when(near_goes(j, ch))
+            def _(j=j, ch=ch):
                 near(j, ch).wait_send()
-        for ch in range(CHUNKS):
+
             @pl.when(relays(j, ch))
             def _(j=j, ch=ch):
                 relay(j, ch).wait_send()
@@ -376,9 +454,10 @@
         out_specs=vmem,
         scratch_shapes=[
             pltpu.VMEM((REACH + 1, DEPTH, BS), bf16),
+            pltpu.VMEM((CROWS, BS), bf16),
             pltpu.VMEM((2, BS, HALF), f32),
             pltpu.VMEM((LAGS * BS, DEPTH), bf16),
-            pltpu.VMEM((DEPTH, BS), bf16),
+            pltpu.VMEM((DEPTH, 2 * BS), bf16),
             pltpu.VMEM((2 * LAGS, BS), f32),
             pltpu.VMEM((K, 4, XROWS, BS), f32),
             pltpu.VMEM((K, 2, 3, HX + TAIL, BS), bf16),
@@ -388,6 +467,9 @@
             pltpu.SemaphoreType.DMA,
             pltpu.SemaphoreType.DMA((4, CHUNKS)),
             pltpu.SemaphoreType.DMA((2, CHUNKS)),
+            pltpu.SemaphoreType.DMA((CHUNKS,)),
+            pltpu.SemaphoreType.DMA,
+            pltpu.SemaphoreType.DMA,
             pltpu.SemaphoreType.DMA((REACH + 1, CHUNKS)),
             pltpu.SemaphoreType.DMA((4, CHUNKS)),
             pltpu.SemaphoreType.DMA((K, 2, 3)),

time: 84.2 us -> 77.9 us (0.925)
  the two profiles are of different devices: /device:TPU:6 before, /device:TPU:9 now
where the time goes in v3:
time: 77.9 us; the launch traced here: 77.8 us
  Pallas kernels  76.1 us (98%)
  local copies, waits for them, and re-layouts  1.67 us (2%)
    pallas_call x1, Pallas kernels, on_device(): pl.pallas_call(kernel, out_shape=jax.ShapeDtypeStruct((LAGS // BANDS, 1,...  76.1 us
    unnamed x1, local copies, waits for them, and re-layouts  1.67 us

profile of v3, /device:TPU:9, one launch (start us, length us, event | category | flops | bytes accessed | tf_op | source)
XLA Modules:
  0.0 77.8 jit_solution(4094442888664815383)
XLA Ops:
  0.0 76.1 %shard_map.46 = bf16[2,1,4,128,128]{4,3,2,1,0:T(8,128)(2,1)} custom-call(bf16[2048,128]{1,0:T(8,128)(2,1)} %bitcast.2, s32[1,128]{1,0:T(1,128)} %bitcast.3, s32[1,4]{1,0:T(1,128)} %offsets.1, f32[16,64,128]{2,1,0:T(8,128)} %constant.2.clone.tables), custom_call_target="tpu_custom_call" | custom-call | flops 8589934592 | bytes 1048576 | tf_op jit(solution)/shard_map/pallas_call | solution.py:450
  76.1 1.7 %copy.6 = bf16[2,1,4,128,128]{4,3,2,1,0:T(8,128)(2,1)} copy(bf16[2,1,4,128,128]{4,3,2,1,0:T(8,128)(2,1)} %shard_map.46) | data formatting | bytes 524288

commit v4 on v3

--- a/solution.py
+++ b/solution.py
@@ -142,11 +142,24 @@
         for ch in range(CHUNKS):
             far(ch).start()
 
-    for j in (1, 3):
-        @pl.when(y >= j)
-        def _(j=j):
-            for ch in range(CHUNKS):
-                near(j, ch).start()
+    own_turn = [*upper, *range(CHUNKS // 2)]
+    held = jnp.logical_and(z_lo == 1, y == 2)
+    waits = jnp.logical_and(z_lo == 1, y == 1)
+
+    @pl.when(y >= 1)
+    def _():
+        for ch in range(CHUNKS // 2):
+            near(1, ch).start()
+
+    @pl.when(jnp.logical_and(y >= 1, jnp.logical_not(held)))
+    def _():
+        for ch in upper:
+            near(1, ch).start()
+
+    @pl.when(y == 3)
+    def _():
+        for ch in own_turn:
+            near(3, ch).start()
 
     @pl.when(y == 2)
     def _():
@@ -222,9 +235,15 @@
         @pl.when(z_lo == 0)
         def _(s=s):
             take_far(s)
-        take(1, s, early(1, s))
+        take(1, s, early(1, s) if s < CHUNKS // 2 else jnp.logical_and(early(1, s), jnp.logical_not(waits)))
+        take(3, own_turn[s], jnp.logical_and(z_lo == 1, early(3, own_turn[s])))
         if s > 0:
-            take(3, s - 1, jnp.logical_and(early(3, s - 1), y != 1))
+            take(3, s - 1, jnp.logical_and(z_lo == 0, jnp.logical_and(relays(3, s - 1), y != 1)))
+        if s == CHUNKS // 2 - 1:
+            @pl.when(held)
+            def _():
+                for ch in upper:
+                    near(1, ch).start()
         lax.fori_loop(LAGS // 2 + s * LAGS // 8, LAGS // 2 + (s + 1) * LAGS // 8, build, 0)
 
     def sibling_done(j):
@@ -233,7 +252,6 @@
 
     @pl.when(z_lo == 1)
     def _():
-        take(3, CHUNKS - 1, early(3, CHUNKS - 1))
         for ch in range(CHUNKS):
             take(2, ch, early(2, ch))
         for j in range(4):
@@ -241,8 +259,11 @@
             def _(j=j):
                 sibling_done(j)
 
-    def pass_on(ch, here):
-        take(3, ch, jnp.logical_and(z_lo == 0, jnp.logical_and(relays(3, ch), here)))
+    def pass_on(ch, yy):
+        take(3, ch, jnp.logical_and(z_lo == 0, y == yy))
+
+    def take_late(j, ch):
+        take(j, ch, jnp.logical_not(early(j, ch)))
 
     def gather_rest():
         @pl.when(jnp.logical_and(z_lo == 1, y == 3))
@@ -251,9 +272,9 @@
                 aside(ch).wait_recv()
                 aside_on(ch).start()
 
-        for j in (1, 3, 2):
-            for ch in range(CHUNKS):
-                take(j, ch, jnp.logical_not(early(j, ch)))
+        for j in (3, 2):
+            for ch in upper:
+                take_late(j, ch)
         for j in range(4):
             taken = jnp.logical_and(z_lo == 1, jnp.logical_and(core == 0, y == 3 - j))
 
@@ -261,22 +282,18 @@
             def _(j=j):
                 sibling_done(j)
 
-    def middle(k, way):
-        return remote(
-            go.at[k, way, 0], come.at[k, way, 0], x_send.at[k, way, 0], x_recv.at[k, way, 0],
-            x_down if way else x_up,
-        )
-
-    def straight(k, way):
-        return remote(
-            go.at[k, way, 1], come.at[k, way, 1], x_send.at[k, way, 1], x_recv.at[k, way, 1],
-            x_down if way else x_up,
-        )
-
-    def summed(k, way):
-        return remote(
-            go.at[k, way, 2], come.at[k, way, 2], x_send.at[k, way, 2], x_recv.at[k, way, 2],
-            x_down if way else x_up,
+    def pieces_of(k):
+        return 2 if k == K - 1 else 1
+
+    def hop(k, way, kind):
+        used = pl.ds(0, HX)
+        if kind >= 2:
+            size = HX // pieces_of(k) + TAIL
+            used = pl.ds((kind - 2) * size, size)
+        place = min(kind, 2)
+        return remote(
+            go.at[k, way, place, used], come.at[k, way, place, used],
+            x_send.at[k, way, kind], x_recv.at[k, way, kind], x_down if way else x_up,
         )
 
     def z_copy(k, ee):
@@ -299,106 +316,144 @@
             tail = jnp.where(tail_row == lag, jnp.sum(rest, axis=0, keepdims=True), tail)
         message[pl.ds(lags * BS, TAIL), :] = tail.astype(jnp.bfloat16)
 
+    def plain(message, value_of):
+        for lag in range(4):
+            message[pl.ds(lag * BS, BS), :] = value_of(lag).astype(jnp.bfloat16)
+
     def unpack(message, lags, lag):
         tail = message[pl.ds(lags * BS, TAIL), :].astype(jnp.float32)[lag:lag + 1]
         return message[pl.ds(lag * BS, BS), :].astype(jnp.float32) + jnp.where(diagonal, tail, 0.0)
 
-    def part_of(k, q, lag):
-        return part[k, q, pl.ds(lag * BS, BS), :]
-
-    def send_middle(k):
+    def rows_at(place):
+        return pl.ds(pl.multiple_of(place * BS, BS), BS)
+
+    def send_middle(k, way):
+        plain(go.at[k, way, 0], lambda lag: part[k, 0, rows_at(way * 4 + lag), :])
+        hop(k, way, 0).start()
+
+    def send_straight(k, way):
+        plain(go.at[k, way, 1], lambda lag: part[k, 1 + way, rows_at((1 - way) * 4 + lag), :])
+        hop(k, way, 1).start()
+
+    def send_summed(k):
+        count = 4 // pieces_of(k)
+        size = HX // pieces_of(k) + TAIL
+        for piece in range(pieces_of(k)):
+            for way in (0, 1):
+                def both(lag, way=way, at=piece * count):
+                    through = come[k, way, 0, rows_at(at + lag), :].astype(jnp.float32)
+                    return part[k, 1 + way, rows_at(way * 4 + at + lag), :] + through
+
+                if piece == 0:
+                    hop(k, way, 0).wait_recv()
+                pack(go.at[k, way, 2, pl.ds(piece * size, size)], count, both)
+                hop(k, way, 2 + piece).start()
+
+    def reduce_x(k):
+        count = 4 // pieces_of(k)
+        size = HX // pieces_of(k) + TAIL
         for way in (0, 1):
-            pack(go.at[k, way, 0], 4, lambda lag, way=way: part_of(k, 0, way * 4 + lag))
-            middle(k, way).start()
-
-    def send_straight(k, way):
-        pack(go.at[k, way, 1], 4, lambda lag: part_of(k, 1 + way, (1 - way) * 4 + lag))
-        straight(k, way).start()
-
-    def send_summed(k):
-        for way in (0, 1):
-            def both(lag, way=way):
-                return part_of(k, 1 + way, way * 4 + lag) + unpack(come.at[k, way, 0], 4, lag)
-
-            middle(k, way).wait_recv()
-            pack(go.at[k, way, 2], 4, both)
-            summed(k, way).start()
-
-    def multiply(slots, *after):
-        width = len(slots) * BS
-
-        def quarter(q, carry):
-            ahead = jnp.where(q == 0, 2, jnp.where(q == 1, 1, jnp.where(q == 2, 3, 0)))
-            rows = pl.ds(pl.multiple_of((x + ahead) % 4 * XROWS, XROWS), XROWS)
-            total = jnp.dot(left[rows, :], right[:, pl.ds(0, width)], preferred_element_type=jnp.float32)
-            for n, k in enumerate(slots):
-                part[k, q] = total[:, n * BS:(n + 1) * BS]
-            for at, then in enumerate(after):
-                pl.when(q == at)(then)
-            return carry
-
-        lax.fori_loop(0, 4, quarter, 0)
-
-    def reduce_x(k):
-        for way in (0, 1):
-            straight(k, way).wait_recv()
-            summed(k, way).wait_recv()
-        for lag in range(8):
-            up = 2 if lag < 4 else 1
-            total = part_of(k, 3, lag) + unpack(come.at[k, 0, up], 4, lag % 4)
-            part[k, 3, pl.ds(lag * BS, BS), :] = total + unpack(come.at[k, 1, 3 - up], 4, lag % 4)
-        for ee in (2, 1, 3):
-            def to_send(lag, ee=ee):
-                row = ((z_hi + ee) % 4 * 2 + lag) * BS
-                return part[k, 3, pl.ds(pl.multiple_of(row, BS), BS), :]
-
-            pack(zsums.at[k, ee - 1], 2, to_send)
-            z_copy(k, ee).start()
+            hop(k, way, 1).wait_recv()
+        for piece in range(pieces_of(k)):
+            for way in (0, 1):
+                hop(k, way, 2 + piece).wait_recv()
+                for lag in range(count):
+                    at = piece * count + lag
+                    rows = rows_at(way * 4 + at)
+                    straight = come[k, 1 - way, 1, rows_at(at), :].astype(jnp.float32)
+                    summed = unpack(come.at[k, way, 2, pl.ds(piece * size, size)], count, lag)
+                    part[k, 3, rows, :] = part[k, 3, rows, :] + straight + summed
+            if pieces_of(k) == 1:
+                for ee in (2, 1, 3):
+                    send_z(k, ee)
+            else:
+                for e in (piece, 2 + piece):
+                    @pl.when(e != z_hi)
+                    def _(e=e):
+                        send_z(k, (e + 4 - z_hi) % 4)
+
+    def send_z(k, ee):
+        e = (z_hi + ee) % 4
+        pack(zsums.at[k, ee - 1], 2, lambda lag: part[k, 3, rows_at(e * 2 + lag), :])
+        z_copy(k, ee).start()
 
     def finish(k):
         for ee in (1, 3, 2):
             z_copy(k, ee).wait_recv()
         for lag in range(2):
-            total = part[k, 3, pl.ds(pl.multiple_of((z_hi * 2 + lag) * BS, BS), BS), :]
+            total = part[k, 3, rows_at(z_hi * 2 + lag), :]
             for s in range(3):
                 total += unpack(zgot.at[k, s], 2, lag)
             out[lag, 0, k] = (total * SCALE).astype(jnp.bfloat16)
 
+    def pick(t, values):
+        chosen = jnp.int32(values[-1])
+        for at in range(len(values) - 1):
+            chosen = jnp.where(t == at, values[at], chosen)
+        return chosen
+
+    def multiply(slots, *after):
+        width = len(slots) * BS
+
+        def step(t, carry):
+            q = pick(t, (0, 0, 1, 2, 1, 2, 3, 3))
+            high = pick(t, (0, 1, 1, 0, 0, 1, 0, 1))
+            ahead = pick(t, (2, 2, 1, 3, 1, 3, 0, 0))
+            rows = pl.ds(pl.multiple_of(((x + ahead) % 4 * 2 + high) * HX, HX), HX)
+            total = jnp.dot(left[rows, :], right[:, pl.ds(0, width)], preferred_element_type=jnp.float32)
+            for n, k in enumerate(slots):
+                part[k, q, pl.ds(pl.multiple_of(high * HX, HX), HX), :] = total[:, n * BS:(n + 1) * BS]
+            for at, then in enumerate(after):
+                pl.when(t == at)(then)
+            return carry
+
+        lax.fori_loop(0, 8, step, 0)
+
+    def run(*steps):
+        def then():
+            for step in steps:
+                step[0](*step[1:])
+
+        return then
+
     right[:, pl.ds(0, BS)] = blocks[jnp.minimum(REACH, 15 - fibre)]
-    def zero_0():
-        send_middle(0)
-        pass_on(3, y != 1)
-        pass_on(2, y == 1)
-
-    def zero_1():
-        send_straight(0, 0)
-        pass_on(3, y == 1)
-
-    multiply((0,), zero_0, zero_1, lambda: send_straight(0, 1), lambda: send_summed(0))
+    multiply(
+        (0,),
+        run((send_middle, 0, 0), (pass_on, 3, 0)),
+        run((send_middle, 0, 1), (pass_on, 2, 1), (pass_on, 3, 2), (take, 1, 2, waits)),
+        run((send_straight, 0, 0)),
+        run((send_straight, 0, 1), (pass_on, 3, 1), (take, 1, 3, waits)),
+        run(),
+        run((take_late, 3, 0), (take_late, 3, 1)),
+        run(*((take_late, 1, ch) for ch in range(CHUNKS))),
+        run((send_summed, 0), (take_late, 2, 0), (take_late, 2, 1)),
+    )
     gather_rest()
     for n, slot in enumerate((1, 2)):
         right[:, pl.ds(n * BS, BS)] = blocks[offsets[0, slot]]
-
-    def two_3():
-        send_middle(2)
-        send_summed(1)
-        send_straight(2, 0)
-        send_straight(2, 1)
-        reduce_x(0)
-
-    multiply((1, 2), lambda: send_middle(1), lambda: send_straight(1, 0), lambda: send_straight(1, 1), two_3)
+    multiply(
+        (1, 2),
+        run((send_middle, 1, 0)),
+        run((send_middle, 1, 1)),
+        run((send_straight, 1, 0)),
+        run((send_straight, 1, 1)),
+        run((send_middle, 2, 0), (send_middle, 2, 1)),
+        run(),
+        run((send_summed, 1)),
+        run((send_straight, 2, 0), (send_straight, 2, 1), (reduce_x, 0)),
+    )
     right[:, pl.ds(0, BS)] = blocks[offsets[0, 3]]
-
-    def three_0():
-        send_middle(3)
-        send_summed(2)
-
-    def three_3():
-        finish(0)
-        reduce_x(1)
-        send_summed(3)
-
-    multiply((3,), three_0, lambda: send_straight(3, 0), lambda: send_straight(3, 1), three_3)
+    multiply(
+        (3,),
+        run((send_middle, 3, 0)),
+        run((send_middle, 3, 1), (send_summed, 2)),
+        run((send_straight, 3, 0)),
+        run((send_straight, 3, 1), (finish, 0), (reduce_x, 1)),
+        run(),
+        run(),
+        run(),
+        run((send_summed, 3)),
+    )
     reduce_x(2)
     finish(1)
     reduce_x(3)
@@ -437,9 +492,8 @@
 
     for k in range(K):
         for way in (0, 1):
-            middle(k, way).wait_send()
-            straight(k, way).wait_send()
-            summed(k, way).wait_send()
+            for kind in range(2 + pieces_of(k)):
+                hop(k, way, kind).wait_send()
         for ee in (1, 2, 3):
             z_copy(k, ee).wait_send()
 
@@ -460,8 +514,8 @@
             pltpu.VMEM((DEPTH, 2 * BS), bf16),
             pltpu.VMEM((2 * LAGS, BS), f32),
             pltpu.VMEM((K, 4, XROWS, BS), f32),
-            pltpu.VMEM((K, 2, 3, HX + TAIL, BS), bf16),
-            pltpu.VMEM((K, 2, 3, HX + TAIL, BS), bf16),
+            pltpu.VMEM((K, 2, 3, HX + 2 * TAIL, BS), bf16),
+            pltpu.VMEM((K, 2, 3, HX + 2 * TAIL, BS), bf16),
             pltpu.VMEM((K, 3, ZROWS + TAIL, BS), bf16),
             pltpu.VMEM((K, 3, ZROWS + TAIL, BS), bf16),
             pltpu.SemaphoreType.DMA,
@@ -472,8 +526,8 @@
             pltpu.SemaphoreType.DMA,
             pltpu.SemaphoreType.DMA((REACH + 1, CHUNKS)),
             pltpu.SemaphoreType.DMA((4, CHUNKS)),
-            pltpu.SemaphoreType.DMA((K, 2, 3)),
-            pltpu.SemaphoreType.DMA((K, 2, 3)),
+            pltpu.SemaphoreType.DMA((K, 2, 4)),
+            pltpu.SemaphoreType.DMA((K, 2, 4)),
             pltpu.SemaphoreType.DMA((K, 3)),
             pltpu.SemaphoreType.DMA((K, 3)),
         ],

time: 77.9 us -> 75.6 us (0.970); the launches traced: 77.8 us -> 74.2 us
  Pallas kernels: 76.1 us -> 72.5 us
    pallas_call x1, Pallas kernels: 76.1 us -> 72.5 us  [on_device(): pl.pallas_call(kernel, out_shape=jax.ShapeDtypeStruct((LAGS // BANDS, 1,...]
where the time goes in v4:
time: 75.6 us; the launch traced here: 74.2 us
  Pallas kernels  72.5 us (96%)
  local copies, waits for them, and re-layouts  1.67 us (2%)
    pallas_call x1, Pallas kernels, on_device(): pl.pallas_call(kernel, out_shape=jax.ShapeDtypeStruct((LAGS // BANDS, 1,...  72.5 us
    unnamed x1, local copies, waits for them, and re-layouts  1.67 us

profile of v4, /device:TPU:9, one launch (start us, length us, event | category | flops | bytes accessed | tf_op | source)
XLA Modules:
  0.0 74.2 jit_solution(4549687091429356277)
XLA Ops:
  0.0 72.5 %shard_map.46 = bf16[2,1,4,128,128]{4,3,2,1,0:T(8,128)(2,1)} custom-call(bf16[2048,128]{1,0:T(8,128)(2,1)} %bitcast.2, s32[1,128]{1,0:T(1,128)} %bitcast.3, s32[1,4]{1,0:T(1,128)} %offsets.1, f32[16,64,128]{2,1,0:T(8,128)} %constant.2.clone.tables), custom_call_target="tpu_custom_call" | custom-call | flops 8589934592 | bytes 1048576 | tf_op jit(solution)/shard_map/pallas_call | solution.py:504
  72.5 1.7 %copy.6 = bf16[2,1,4,128,128]{4,3,2,1,0:T(8,128)(2,1)} copy(bf16[2,1,4,128,128]{4,3,2,1,0:T(8,128)(2,1)} %shard_map.46) | data formatting | bytes 524288

commit v5 on v4

--- a/solution.py
+++ b/solution.py
@@ -40,7 +40,7 @@
 
 def kernel(
     spectra, mask, offsets, tables, out,
-    blocks, spare, turned, left, right, table, part, go, come, zsums, zgot,
+    raw, done, raw_sem, done_sem, blocks, spare, turned, left, right, table, part, go, come, zsums, zgot,
     table_sem, gather_send, relay_send, aside_send, around_send, around_recv, gather_recv, sib_send, x_send, x_recv, z_send, z_recv,
 ):
     fibre, band = lax.axis_index("fibre"), lax.axis_index("band")
@@ -58,6 +58,8 @@
     other_z = at_fibre(1 - z_lo, y, core)
     y_down, y_up = at_fibre(z_lo, (y + 3) % 4, core), at_fibre(z_lo, (y + 1) % 4, core)
     x_down, x_up = at_band((x + 3) % 4, z_hi), at_band((x + 1) % 4, z_hi)
+    raw_copy = pltpu.make_async_copy(spectra, raw, raw_sem)
+    raw_copy.start()
     barrier = pltpu.get_barrier_semaphore()
     peers = [sibling, other_z, y_down, y_up, x_down, x_up]
     peers += [at_band(x, (z_hi + j) % 4) for j in (1, 2, 3)]
@@ -67,7 +69,8 @@
     table_copy = pltpu.make_async_copy(tables.at[band], table, table_sem)
     table_copy.start()
     alive = mask[...].astype(jnp.bfloat16)
-    blocks[0] = spectra[...] * alive
+    raw_copy.wait()
+    blocks[0] = raw[...] * alive
     pl.semaphore_wait(barrier, len(peers))
 
     def remote(src, dst, send, recv, device):
@@ -330,6 +333,10 @@
     def send_middle(k, way):
         plain(go.at[k, way, 0], lambda lag: part[k, 0, rows_at(way * 4 + lag), :])
         hop(k, way, 0).start()
+
+    def sent(k, kind):
+        for way in (0, 1):
+            hop(k, way, kind).wait_send()
 
     def send_straight(k, way):
         plain(go.at[k, way, 1], lambda lag: part[k, 1 + way, rows_at((1 - way) * 4 + lag), :])
@@ -377,6 +384,9 @@
         pack(zsums.at[k, ee - 1], 2, lambda lag: part[k, 3, rows_at(e * 2 + lag), :])
         z_copy(k, ee).start()
 
+    def give(lag, k):
+        return pltpu.make_async_copy(done.at[lag, k], out.at[lag, 0, k], done_sem.at[lag, k])
+
     def finish(k):
         for ee in (1, 3, 2):
             z_copy(k, ee).wait_recv()
@@ -384,7 +394,8 @@
             total = part[k, 3, rows_at(z_hi * 2 + lag), :]
             for s in range(3):
                 total += unpack(zgot.at[k, s], 2, lag)
-            out[lag, 0, k] = (total * SCALE).astype(jnp.bfloat16)
+            done[lag, k] = (total * SCALE).astype(jnp.bfloat16)
+            give(lag, k).start()
 
     def pick(t, values):
         chosen = jnp.int32(values[-1])
@@ -445,16 +456,15 @@
     right[:, pl.ds(0, BS)] = blocks[offsets[0, 3]]
     multiply(
         (3,),
-        run((send_middle, 3, 0)),
-        run((send_middle, 3, 1), (send_summed, 2)),
-        run((send_straight, 3, 0)),
-        run((send_straight, 3, 1), (finish, 0), (reduce_x, 1)),
         run(),
+        run((send_summed, 2), (reduce_x, 1), (sent, 2, 1), (send_middle, 3, 0), (send_middle, 3, 1)),
         run(),
+        run((sent, 2, 2), (send_straight, 3, 0), (send_straight, 3, 1)),
+        run((reduce_x, 2)),
         run(),
+        run((finish, 0)),
         run((send_summed, 3)),
     )
-    reduce_x(2)
     finish(1)
     reduce_x(3)
     finish(2)
@@ -493,9 +503,12 @@
     for k in range(K):
         for way in (0, 1):
             for kind in range(2 + pieces_of(k)):
-                hop(k, way, kind).wait_send()
+                if k != 2 or kind == 0:
+                    hop(k, way, kind).wait_send()
         for ee in (1, 2, 3):
             z_copy(k, ee).wait_send()
+        for lag in range(2):
+            give(lag, k).wait()
 
 
 def on_device(spectra, dead_mask, partner_offset):
@@ -504,9 +517,13 @@
     return pl.pallas_call(
         kernel,
         out_shape=jax.ShapeDtypeStruct((LAGS // BANDS, 1, K, BS, BS), bf16),
-        in_specs=[vmem, vmem, pl.BlockSpec(memory_space=pltpu.SMEM), pl.BlockSpec(memory_space=pl.ANY)],
-        out_specs=vmem,
+        in_specs=[pl.BlockSpec(memory_space=pl.ANY), vmem, pl.BlockSpec(memory_space=pltpu.SMEM), pl.BlockSpec(memory_space=pl.ANY)],
+        out_specs=pl.BlockSpec(memory_space=pl.ANY),
         scratch_shapes=[
+            pltpu.VMEM((DEPTH, BS), bf16),
+            pltpu.VMEM((LAGS // BANDS, K, BS, BS), bf16),
+            pltpu.SemaphoreType.DMA,
+            pltpu.SemaphoreType.DMA((LAGS // BANDS, K)),
             pltpu.VMEM((REACH + 1, DEPTH, BS), bf16),
             pltpu.VMEM((CROWS, BS), bf16),
             pltpu.VMEM((2, BS, HALF), f32),

time: 75.6 us -> 72.3 us (0.956); the launches traced: 74.2 us -> 72.2 us
  Pallas kernels: 72.5 us -> 70.5 us
    pallas_call x1, Pallas kernels: 72.5 us -> 70.5 us  [on_device(): pl.pallas_call(kernel, out_shape=jax.ShapeDtypeStruct((LAGS // BANDS, 1,...]
where the time goes in v5:
time: 72.3 us; the launch traced here: 72.2 us
  Pallas kernels  70.5 us (98%)
  local copies, waits for them, and re-layouts  1.67 us (2%)
    pallas_call x1, Pallas kernels, on_device(): pl.pallas_call(kernel, out_shape=jax.ShapeDtypeStruct((LAGS // BANDS, 1,...  70.5 us
    unnamed x1, local copies, waits for them, and re-layouts  1.67 us

profile of v5, /device:TPU:9, one launch (start us, length us, event | category | flops | bytes accessed | tf_op | source)
XLA Modules:
  0.0 72.2 jit_solution(13752191479981997434)
XLA Ops:
  0.0 70.5 %shard_map.46 = bf16[2,1,4,128,128]{4,3,2,1,0:T(8,128)(2,1)} custom-call(bf16[2048,128]{1,0:T(8,128)(2,1)} %bitcast.2, s32[1,128]{1,0:T(1,128)} %bitcast.3, s32[1,4]{1,0:T(1,128)} %offsets.1, f32[16,64,128]{2,1,0:T(8,128)} %constant.2.clone.tables), custom_call_target="tpu_custom_call" | custom-call | flops 8589934592 | bytes 1048576 | tf_op jit(solution)/shard_map/pallas_call | solution.py:517
  70.5 1.7 %copy.6 = bf16[2,1,4,128,128]{4,3,2,1,0:T(8,128)(2,1)} copy(bf16[2,1,4,128,128]{4,3,2,1,0:T(8,128)(2,1)} %shard_map.46) | data formatting | bytes 524288

commit v6 on v5

--- a/solution.py
+++ b/solution.py
@@ -1,3 +1,4 @@
+import functools
 import math
 
 import jax
@@ -129,11 +130,16 @@
         return remote(spare, blocks.at[4, last_rows], around_send, gather_recv.at[4, CHUNKS - 1], y_up)
 
     def relays(j, ch):
-        first = ch < CHUNKS // 2
+        last = ch == CHUNKS - 1
+        low = z_lo == 0
         if j == 1:
-            goes = y >= 1 if first else jnp.logical_and(y == 1, ch < CHUNKS - 1)
+            goes = [jnp.logical_and(y >= 1, not last)]
+            if ch == 2:
+                goes = [jnp.logical_or(y == 1, jnp.logical_and(low, y >= 2))]
         else:
-            goes = y == 2 if first else y <= 2
+            goes = [y == 2, jnp.logical_and(y == 0, jnp.logical_or(last, jnp.logical_and(ch == 2, jnp.logical_not(low))))]
+            goes.append(jnp.logical_and(y == 1, last))
+        goes = functools.reduce(jnp.logical_or, goes)
         return jnp.logical_and(chip + j <= 7, goes)
 
     def near_goes(j, ch):
@@ -229,16 +235,11 @@
     table_copy.wait()
     lax.fori_loop(0, LAGS // 2, build, 0)
 
-    @pl.when(y == 3)
-    def _():
-        around().wait_recv()
-        around_on().start()
-
     for s in range(CHUNKS):
         @pl.when(z_lo == 0)
         def _(s=s):
             take_far(s)
-        take(1, s, early(1, s) if s < CHUNKS // 2 else jnp.logical_and(early(1, s), jnp.logical_not(waits)))
+        take(1, s, early(1, s) if s < CHUNKS // 2 else jnp.logical_and(early(1, s), jnp.logical_not(jnp.logical_or(waits, y >= 3 - (z_lo == 0).astype(jnp.int32)))))
         take(3, own_turn[s], jnp.logical_and(z_lo == 1, early(3, own_turn[s])))
         if s > 0:
             take(3, s - 1, jnp.logical_and(z_lo == 0, jnp.logical_and(relays(3, s - 1), y != 1)))
@@ -249,6 +250,11 @@
                     near(1, ch).start()
         lax.fori_loop(LAGS // 2 + s * LAGS // 8, LAGS // 2 + (s + 1) * LAGS // 8, build, 0)
 
+    @pl.when(y == 3)
+    def _():
+        around().wait_recv()
+        around_on().start()
+
     def sibling_done(j):
         for ch in range(CHUNKS):
             across(j, ch).wait_recv()
@@ -275,8 +281,8 @@
                 aside(ch).wait_recv()
                 aside_on(ch).start()
 
-        for j in (3, 2):
-            for ch in upper:
+        for j in (1, 3, 2):
+            for ch in range(CHUNKS):
                 take_late(j, ch)
         for j in range(4):
             taken = jnp.logical_and(z_lo == 1, jnp.logical_and(core == 0, y == 3 - j))
@@ -430,14 +436,14 @@
     right[:, pl.ds(0, BS)] = blocks[jnp.minimum(REACH, 15 - fibre)]
     multiply(
         (0,),
-        run((send_middle, 0, 0), (pass_on, 3, 0)),
-        run((send_middle, 0, 1), (pass_on, 2, 1), (pass_on, 3, 2), (take, 1, 2, waits)),
+        run((send_middle, 0, 0), (pass_on, 3, 0), (take, 1, 2, jnp.logical_and(z_lo == 0, y >= 2))),
+        run((send_middle, 0, 1), (pass_on, 3, 2), (take, 1, 2, waits)),
         run((send_straight, 0, 0)),
         run((send_straight, 0, 1), (pass_on, 3, 1), (take, 1, 3, waits)),
         run(),
-        run((take_late, 3, 0), (take_late, 3, 1)),
-        run(*((take_late, 1, ch) for ch in range(CHUNKS))),
-        run((send_summed, 0), (take_late, 2, 0), (take_late, 2, 1)),
+        run(),
+        run(),
+        run((send_summed, 0)),
     )
     gather_rest()
     for n, slot in enumerate((1, 2)):

time: 72.3 us -> 71 us (0.982)
  Pallas kernels: 70.5 us -> 69.1 us
    pallas_call x1, Pallas kernels: 70.5 us -> 69.1 us  [on_device(): pl.pallas_call(kernel, out_shape=jax.ShapeDtypeStruct((LAGS // BANDS, 1,...]
where the time goes in v6:
time: 71 us; the launch traced here: 70.8 us
  Pallas kernels  69.1 us (97%)
  local copies, waits for them, and re-layouts  1.67 us (2%)
    pallas_call x1, Pallas kernels, on_device(): pl.pallas_call(kernel, out_shape=jax.ShapeDtypeStruct((LAGS // BANDS, 1,...  69.1 us
    unnamed x1, local copies, waits for them, and re-layouts  1.67 us

profile of v6, /device:TPU:9, one launch (start us, length us, event | category | flops | bytes accessed | tf_op | source)
XLA Modules:
  0.0 70.8 jit_solution(4922768143846326377)
XLA Ops:
  0.0 69.1 %shard_map.46 = bf16[2,1,4,128,128]{4,3,2,1,0:T(8,128)(2,1)} custom-call(bf16[2048,128]{1,0:T(8,128)(2,1)} %bitcast.2, s32[1,128]{1,0:T(1,128)} %bitcast.3, s32[1,4]{1,0:T(1,128)} %offsets.1, f32[16,64,128]{2,1,0:T(8,128)} %constant.2.clone.tables), custom_call_target="tpu_custom_call" | custom-call | flops 8589934592 | bytes 1048576 | tf_op jit(solution)/shard_map/pallas_call | solution.py:523
  69.1 1.7 %copy.6 = bf16[2,1,4,128,128]{4,3,2,1,0:T(8,128)(2,1)} copy(bf16[2,1,4,128,128]{4,3,2,1,0:T(8,128)(2,1)} %shard_map.46) | data formatting | bytes 524288

commit v7 on v6

--- a/solution.py
+++ b/solution.py
@@ -294,16 +294,16 @@
     def pieces_of(k):
         return 2 if k == K - 1 else 1
 
-    def hop(k, way, kind):
-        used = pl.ds(0, HX)
-        if kind >= 2:
-            size = HX // pieces_of(k) + TAIL
-            used = pl.ds((kind - 2) * size, size)
-        place = min(kind, 2)
-        return remote(
-            go.at[k, way, place, used], come.at[k, way, place, used],
-            x_send.at[k, way, kind], x_recv.at[k, way, kind], x_down if way else x_up,
-        )
+    def hop(k, way, kind, piece=0):
+        rows, rest = HX // pieces_of(k), TAIL if kind == 2 else 0
+        used = pl.ds(0, HX) if kind == 0 else pl.ds(piece * (rows + rest), rows + rest)
+        return remote(
+            go.at[k, way, kind, used], come.at[k, way, kind, used],
+            x_send.at[k, way, kind, piece], x_recv.at[k, way, kind, piece], x_down if way else x_up,
+        )
+
+    def hops_of(k):
+        return [(0, 0)] + [(kind, piece) for kind in (1, 2) for piece in range(pieces_of(k))]
 
     def z_copy(k, ee):
         return remote(
@@ -344,32 +344,33 @@
         for way in (0, 1):
             hop(k, way, kind).wait_send()
 
-    def send_straight(k, way):
-        plain(go.at[k, way, 1], lambda lag: part[k, 1 + way, rows_at((1 - way) * 4 + lag), :])
-        hop(k, way, 1).start()
-
-    def send_summed(k):
+    def send_straight(k, way, piece=0):
+        if piece == 0:
+            plain(go.at[k, way, 1], lambda lag: part[k, 1 + way, rows_at((1 - way) * 4 + lag), :])
+        hop(k, way, 1, piece).start()
+
+    def send_summed(k, piece=0):
+        count = 4 // pieces_of(k)
+        size = HX // pieces_of(k) + TAIL
+        for way in (0, 1):
+            def both(lag, way=way):
+                at = piece * count + lag
+                through = come[k, way, 0, rows_at(at), :].astype(jnp.float32)
+                return part[k, 1 + way, rows_at(way * 4 + at), :] + through
+
+            if piece == 0:
+                hop(k, way, 0).wait_recv()
+            pack(go.at[k, way, 2, pl.ds(piece * size, size)], count, both)
+            hop(k, way, 2, piece).start()
+
+    def reduce_x(k):
         count = 4 // pieces_of(k)
         size = HX // pieces_of(k) + TAIL
         for piece in range(pieces_of(k)):
             for way in (0, 1):
-                def both(lag, way=way, at=piece * count):
-                    through = come[k, way, 0, rows_at(at + lag), :].astype(jnp.float32)
-                    return part[k, 1 + way, rows_at(way * 4 + at + lag), :] + through
-
-                if piece == 0:
-                    hop(k, way, 0).wait_recv()
-                pack(go.at[k, way, 2, pl.ds(piece * size, size)], count, both)
-                hop(k, way, 2 + piece).start()
-
-    def reduce_x(k):
-        count = 4 // pieces_of(k)
-        size = HX // pieces_of(k) + TAIL
-        for way in (0, 1):
-            hop(k, way, 1).wait_recv()
-        for piece in range(pieces_of(k)):
+                hop(k, way, 1, piece).wait_recv()
+                hop(k, way, 2, piece).wait_recv()
             for way in (0, 1):
-                hop(k, way, 2 + piece).wait_recv()
                 for lag in range(count):
                     at = piece * count + lag
                     rows = rows_at(way * 4 + at)
@@ -465,11 +466,11 @@
         run(),
         run((send_summed, 2), (reduce_x, 1), (sent, 2, 1), (send_middle, 3, 0), (send_middle, 3, 1)),
         run(),
-        run((sent, 2, 2), (send_straight, 3, 0), (send_straight, 3, 1)),
-        run((reduce_x, 2)),
+        run((send_straight, 3, 0), (send_straight, 3, 1)),
+        run((sent, 2, 2), (reduce_x, 2)),
         run(),
         run((finish, 0)),
-        run((send_summed, 3)),
+        run((send_summed, 3, 0), (send_straight, 3, 0, 1), (send_straight, 3, 1, 1), (send_summed, 3, 1)),
     )
     finish(1)
     reduce_x(3)
@@ -508,9 +509,9 @@
 
     for k in range(K):
         for way in (0, 1):
-            for kind in range(2 + pieces_of(k)):
+            for kind, piece in hops_of(k):
                 if k != 2 or kind == 0:
-                    hop(k, way, kind).wait_send()
+                    hop(k, way, kind, piece).wait_send()
         for ee in (1, 2, 3):
             z_copy(k, ee).wait_send()
         for lag in range(2):
@@ -549,8 +550,8 @@
             pltpu.SemaphoreType.DMA,
             pltpu.SemaphoreType.DMA((REACH + 1, CHUNKS)),
             pltpu.SemaphoreType.DMA((4, CHUNKS)),
-            pltpu.SemaphoreType.DMA((K, 2, 4)),
-            pltpu.SemaphoreType.DMA((K, 2, 4)),
+            pltpu.SemaphoreType.DMA((K, 2, 3, 2)),
+            pltpu.SemaphoreType.DMA((K, 2, 3, 2)),
             pltpu.SemaphoreType.DMA((K, 3)),
             pltpu.SemaphoreType.DMA((K, 3)),
         ],

time: 71 us -> 71 us (level)
  no operation moved by 1% of the time
where the time goes in v7:
time: 71 us; the launch traced here: 70.8 us
  Pallas kernels  69.2 us (97%)
  local copies, waits for them, and re-layouts  1.67 us (2%)
    pallas_call x1, Pallas kernels, on_device(): pl.pallas_call(kernel, out_shape=jax.ShapeDtypeStruct((LAGS // BANDS, 1,...  69.2 us
    unnamed x1, local copies, waits for them, and re-layouts  1.67 us

profile of v7, /device:TPU:9, one launch (start us, length us, event | category | flops | bytes accessed | tf_op | source)
XLA Modules:
  0.0 70.8 jit_solution(2271922445699610817)
XLA Ops:
  0.0 69.2 %shard_map.46 = bf16[2,1,4,128,128]{4,3,2,1,0:T(8,128)(2,1)} custom-call(bf16[2048,128]{1,0:T(8,128)(2,1)} %bitcast.2, s32[1,128]{1,0:T(1,128)} %bitcast.3, s32[1,4]{1,0:T(1,128)} %offsets.1, f32[16,64,128]{2,1,0:T(8,128)} %constant.2.clone.tables), custom_call_target="tpu_custom_call" | custom-call | flops 8589934592 | bytes 1048576 | tf_op jit(solution)/shard_map/pallas_call | solution.py:524
  69.2 1.7 %copy.6 = bf16[2,1,4,128,128]{4,3,2,1,0:T(8,128)(2,1)} copy(bf16[2,1,4,128,128]{4,3,2,1,0:T(8,128)(2,1)} %shard_map.46) | data formatting | bytes 524288

commit v8 on v7

--- a/solution.py
+++ b/solution.py
@@ -456,9 +456,9 @@
         run((send_straight, 1, 0)),
         run((send_straight, 1, 1)),
         run((send_middle, 2, 0), (send_middle, 2, 1)),
-        run(),
+        run((reduce_x, 0)),
         run((send_summed, 1)),
-        run((send_straight, 2, 0), (send_straight, 2, 1), (reduce_x, 0)),
+        run((send_straight, 2, 0), (send_straight, 2, 1)),
     )
     right[:, pl.ds(0, BS)] = blocks[offsets[0, 3]]
     multiply(

time: 71 us -> 71.2 us (level)
  no operation moved by 1% of the time
where the time goes in v8:
time: 71.2 us; the launch traced here: 71.1 us
  Pallas kernels  69.4 us (97%)
  local copies, waits for them, and re-layouts  1.67 us (2%)
    pallas_call x1, Pallas kernels, on_device(): pl.pallas_call(kernel, out_shape=jax.ShapeDtypeStruct((LAGS // BANDS, 1,...  69.4 us
    unnamed x1, local copies, waits for them, and re-layouts  1.67 us

profile of v8, /device:TPU:9, one launch (start us, length us, event | category | flops | bytes accessed | tf_op | source)
XLA Modules:
  0.0 71.1 jit_solution(5491858488198953861)
XLA Ops:
  0.0 69.4 %shard_map.46 = bf16[2,1,4,128,128]{4,3,2,1,0:T(8,128)(2,1)} custom-call(bf16[2048,128]{1,0:T(8,128)(2,1)} %bitcast.2, s32[1,128]{1,0:T(1,128)} %bitcast.3, s32[1,4]{1,0:T(1,128)} %offsets.1, f32[16,64,128]{2,1,0:T(8,128)} %constant.2.clone.tables), custom_call_target="tpu_custom_call" | custom-call | flops 8589934592 | bytes 1048576 | tf_op jit(solution)/shard_map/pallas_call | solution.py:524
  69.4 1.7 %copy.6 = bf16[2,1,4,128,128]{4,3,2,1,0:T(8,128)(2,1)} copy(bf16[2,1,4,128,128]{4,3,2,1,0:T(8,128)(2,1)} %shard_map.46) | data formatting | bytes 524288
